TPU v7x, 512 devices: a whole 4x8x8 slice. The times are simulated.
512 devices in a mesh: dom: 128 (over y, z, core), cuts: 4 (over x).
Axes of the slice: x: 4, y: 8, z: 8, core: 2. Of those that a mesh axis runs over, the one named last changes fastest.
Arguments:
- features: bfloat16 [196608, 128], P(('dom', 'cuts')), may hold values from -6 to 6
- weight_one: bfloat16 [128, 256], replicated, may hold values from -0.5 to 0.5
- bias_one: float32 [256], replicated, may hold values from -3 to 3
- weight_two: bfloat16 [256, 256], replicated, may hold values from -0.375 to 0.375
- bias_two: float32 [256], replicated, may hold values from -3 to 3
- hub_rows: int32 [128, 4, 16], P('dom', 'cuts'), may hold values from 0 to 383, as said below
- halo_rows: int32 [128, 4, 128, 16], P('dom', 'cuts'), may hold values from 0 to 383
- halo_count: int32 [128, 4, 128], P('dom', 'cuts'), may hold values from 0 to 16, as said below
- tile_target: int32 [128, 4, 16], P('dom', 'cuts'), may hold values from 0 to 11
- tile_source: int32 [128, 4, 16], P('dom', 'cuts'), may hold values from 0 to 34
- tile_count: int32 [128, 4], P('dom', 'cuts'), may hold values from 4 to 16, as said below
- tile_values: bfloat16 [128, 4, 16, 128, 128], P('dom', 'cuts'), may hold values from -0.25 to 0.25
Outputs:
- hidden_two: bfloat16 [196608, 256], P(('dom', 'cuts'))
Inputs may be any that keep to these rules, and one draw needn't show every extreme that they name: `hub_rows`: the 16 rows of each slice are distinct. `halo_count`: A partition sends nothing to itself (count 0); some pair uses all 16 rows. `tile_count`: some slice uses all 16 tiles.
All inputs are finite; a program needn't handle non-finite values.
Results may differ from a plain program's by a relative error of at most 0.0054.
Values may be sent and summed in bfloat16 or wider, within the bound.
No kernel may reach another device: no remote copies, remote signals or barrier semaphores. Data moves between devices by JAX's collectives and lax.ppermute only.
A program may use at most 64 MiB of HBM per device.

v0:
```python
import jax
import jax.numpy as jnp
from jax import lax
from jax.sharding import PartitionSpec as P

ROWS_DEV = 384


def collect(table, halo_rows, halo_count, hub_rows):
    width = table.shape[1]
    picks = halo_rows[0, 0]
    slot_len = picks.shape[1]
    live_slots = jnp.arange(slot_len, dtype=jnp.int32)[None, :] < halo_count[0, 0][:, None]
    outgoing = jnp.where(live_slots[..., None], table[picks], jnp.zeros((), table.dtype))
    hub_local = table[hub_rows[0, 0]]
    halo_in = lax.all_to_all(outgoing, "dom", split_axis=0, concat_axis=0, tiled=True).reshape(
        -1, width
    )
    hubs_in = lax.all_gather(hub_local, "dom", axis=0, tiled=True)
    return jnp.concatenate([table, halo_in, hubs_in], axis=0)


def aggregate(sources, tile_target, tile_source, tile_count, tile_values, bias):
    block = tile_values.shape[-1]
    width = sources.shape[1]
    blocks = sources.reshape(-1, block, width)
    tiles = tile_values[0, 0]
    targets = tile_target[0, 0]
    columns = tile_source[0, 0]
    count_used = tile_count[0, 0]
    capacity = tiles.shape[0]
    row_blocks = ROWS_DEV * lax.axis_size("cuts") // block

    def group_sum(group_index, totals):
        start = group_index * capacity
        picked = blocks[columns]
        products = jnp.einsum("tij,tjf->tif", tiles, picked, preferred_element_type=jnp.float32)
        live_tiles = start + jnp.arange(capacity, dtype=jnp.int32) < count_used
        products = jnp.where(live_tiles[:, None, None], products, jnp.zeros((), jnp.float32))
        return totals.at[targets].add(products)

    empty = jnp.zeros((row_blocks, block, width), jnp.float32)
    totals = lax.fori_loop(0, capacity // capacity, group_sum, empty)
    partial_sums = totals.reshape(row_blocks * block, width)
    summed = lax.psum_scatter(partial_sums, "cuts", scatter_dimension=0, tiled=True)
    return jax.nn.relu(summed + bias[None, :]).astype(jnp.bfloat16)


def local(
    features,
    weight_one,
    bias_one,
    weight_two,
    bias_two,
    hub_rows,
    halo_rows,
    halo_count,
    tile_target,
    tile_source,
    tile_count,
    tile_values,
):
    proj_one = jnp.dot(features, weight_one, preferred_element_type=jnp.float32).astype(
        jnp.bfloat16
    )
    sources_one = collect(proj_one, halo_rows, halo_count, hub_rows)
    hidden_one = aggregate(sources_one, tile_target, tile_source, tile_count, tile_values, bias_one)
    proj_two = jnp.dot(hidden_one, weight_two, preferred_element_type=jnp.float32).astype(
        jnp.bfloat16
    )
    sources_two = collect(proj_two, halo_rows, halo_count, hub_rows)
    return aggregate(sources_two, tile_target, tile_source, tile_count, tile_values, bias_two)


def solution(mesh):
    return jax.shard_map(
        local,
        mesh=mesh,
        in_specs=(
            P(("dom", "cuts"), None),
            P(),
            P(),
            P(),
            P(),
            P("dom", "cuts", None),
            P("dom", "cuts", None, None),
            P("dom", "cuts", None),
            P("dom", "cuts", None),
            P("dom", "cuts", None),
            P("dom", "cuts"),
            P("dom", "cuts", None, None, None),
        ),
        out_specs=P(("dom", "cuts"), None),
        check_vma=False,
    )
```

profile of v0, /device:TPU:1, one launch (start us, length us, event | category | flops | bytes accessed | tf_op | source)
XLA Modules:
  0.0 295.1 jit_solution(16527121575798713138)
XLA Ops:
  8.4 1.2 gather_fusion.1
  11.2 7.5 %gather_fusion = bf16[2048,256]{1,0:T(8,128)(2,1)S(1)} fusion(bf16[384,256]{1,0:T(8,128)(2,1)S(1)} %convolution_convert_fusion.1, s32[2048]{0:T(1024)S(1)} %broadcast_clamp_fusion), kind=kCustom, calls=%fused_computation | custom fusion | bytes 2105344 | tf_op jit(solution)/shard_map/gather | solution.py:14
  18.7 1.2 broadcast_select_fusion.1
  20.0 18.4 %all-to-all-start = ((bf16[128,16,256]{2,1,0:T(8,128)(2,1)}), bf16[128,16,256]{2,1,0:T(8,128)(2,1)S(1)}, u32[]{:S(2)}, u32[]{:S(2)}) async-start(bf16[128,16,256]{2,1,0:T(8,128)(2,1)} %broadcast_select_fusion.1), calls=%async_computation | async-start | bytes 2097152 | tf_op jit(solution)/shard_map/all_to_all | solution.py:16
  39.2 69.7 %all-gather.5.cloned.1.call-done = bf16[2048,256]{1,0:T(8,128)(2,1)} async-done(((bf16[16,256]{1,0:T(8,128)(2,1)}), bf16[2048,256]{1,0:T(8,128)(2,1)}) %all-gather.5.cloned.1.call-update) | async-done | bytes 1048592 | tf_op jit(solution)/shard_map/all_gather | solution.py:19
  109.9 1.7 pad_maximum_fusion
  111.6 1.6 gather_fusion.2
  113.2 1.7 select_bitcast_fusion.1
  114.9 1.8 copy.17
  116.9 3.5 %scatter_fusion = f32[12,128,256]{2,1,0:T(8,128)S(1)} fusion(f32[12,128,256]{2,1,0:T(8,128)S(1)} %broadcast.111.clone, s32[16]{0:T(128)S(1)} %fusion.4, f32[16,128,256]{2,1,0:T(8,128)} %copy.17), kind=kCustom, calls=%fused_computation.6 | custom fusion | flops 524288 | bytes 6291520 | tf_op jit(solution)/shard_map/while/body/eval_jaxpr/scatter-add | solution.py:40
  121.6 25.4 %reduce-scatter.3.cloned.1.call-done = f32[384,256]{1,0:T(8,128)} async-done(((f32[1536,256]{1,0:T(8,128)}), f32[384,256]{1,0:T(8,128)}) %reduce-scatter.3.cloned.1.call-update) | async-done | bytes 393232 | tf_op jit(solution)/shard_map/reduce_scatter | solution.py:45
  147.0 1.2 convolution_convert_fusion
  148.2 1.2 gather_fusion.4
  149.4 7.5 %gather_fusion.3 = bf16[2048,256]{1,0:T(8,128)(2,1)S(1)} fusion(bf16[384,256]{1,0:T(8,128)(2,1)S(1)} %convolution_convert_fusion, s32[2048]{0:T(1024)S(1)} %broadcast_clamp_fusion), kind=kCustom, calls=%fused_computation.3 | custom fusion | bytes 2105344 | tf_op jit(solution)/shard_map/gather | solution.py:14
  156.9 1.2 broadcast_select_fusion
  158.2 15.3 %all-to-all-start.1 = ((bf16[128,16,256]{2,1,0:T(8,128)(2,1)}), bf16[128,16,256]{2,1,0:T(8,128)(2,1)S(1)}, u32[]{:S(2)}, u32[]{:S(2)}) async-start(bf16[128,16,256]{2,1,0:T(8,128)(2,1)} %broadcast_select_fusion), calls=%async_computation.2 | async-start | bytes 2097152 | tf_op jit(solution)/shard_map/all_to_all | solution.py:16
  173.5 75.2 %all-gather.7.cloned.1.call-done = bf16[2048,256]{1,0:T(8,128)(2,1)} async-done(((bf16[16,256]{1,0:T(8,128)(2,1)}), bf16[2048,256]{1,0:T(8,128)(2,1)}) %all-gather.7.cloned.1.call-update) | async-done | bytes 1048592 | tf_op jit(solution)/shard_map/all_gather | solution.py:19
  249.7 1.7 pad_maximum_fusion.1
  251.4 1.6 gather_fusion.5
  253.0 1.7 select_bitcast_fusion
  254.7 1.8 copy.19
  256.7 3.5 %scatter_fusion.1 = f32[12,128,256]{2,1,0:T(8,128)S(1)} fusion(f32[12,128,256]{2,1,0:T(8,128)S(1)} %broadcast.111, s32[16]{0:T(128)S(1)} %fusion.4, f32[16,128,256]{2,1,0:T(8,128)} %copy.19), kind=kCustom, calls=%fused_computation.7 | custom fusion | flops 524288 | bytes 6291520 | tf_op jit(solution)/shard_map/while/body/eval_jaxpr/scatter-add | solution.py:40
  261.4 25.4 %reduce-scatter.5.cloned.1.call-done = f32[384,256]{1,0:T(8,128)} async-done(((f32[1536,256]{1,0:T(8,128)}), f32[384,256]{1,0:T(8,128)}) %reduce-scatter.5.cloned.1.call-update) | async-done | bytes 393232 | tf_op jit(solution)/shard_map/reduce_scatter | solution.py:45
  286.8 1.7 maximum_convert_fusion
  (44 shorter events, 8.3 us)
Async XLA Ops:
  6.5 106.6 %copy-start = (bf16[1,1,16,128,128]{4,3,2,1,0:T(8,128)(2,1)S(1)}, bf16[1,1,16,128,128]{4,3,2,1,0:T(8,128)(2,1)}, u32[]{:S(2)}) copy-start(bf16[1,1,16,128,128]{4,3,2,1,0:T(8,128)(2,1)} %param.23) | copy-start | bytes 1572868
  6.5 102.3 %all-gather.5.cloned.1.call-start = ((), (), s32[]{:S(2)}) async-start(), calls=%async_computation.6 | async-start | bytes 1056768 | tf_op jit(solution)/shard_map/all_gather | solution.py:19
  18.7 20.4 %copy-start.8 = (s32[1,1,16]{2,1,0:T(1,128)S(1)}, s32[1,1,16]{2,1,0:T(1,128)}, u32[]{:S(2)}) copy-start(s32[1,1,16]{2,1,0:T(1,128)} %param.21) | copy-start | bytes 196
  18.7 20.4 %copy-start.9 = (s32[1,1,16]{2,1,0:T(1,128)S(1)}, s32[1,1,16]{2,1,0:T(1,128)}, u32[]{:S(2)}) copy-start(s32[1,1,16]{2,1,0:T(1,128)} %param.20) | copy-start | bytes 196
  20.0 88.9 %all-to-all-start = ((bf16[128,16,256]{2,1,0:T(8,128)(2,1)}), bf16[128,16,256]{2,1,0:T(8,128)(2,1)S(1)}, u32[]{:S(2)}, u32[]{:S(2)}) async-start(bf16[128,16,256]{2,1,0:T(8,128)(2,1)} %broadcast_select_fusion.1), calls=%async_computation | async-start | bytes 2097152 | tf_op jit(solution)/shard_map/all_to_all | solution.py:16
  38.4 108.6 %reduce-scatter.3.cloned.1.call-start = ((), (), s32[]{:S(2)}) async-start(), calls=%async_computation.4 | async-start | bytes 1966080 | tf_op jit(solution)/shard_map/reduce_scatter | solution.py:45
  108.9 1.0 copy-start.3
  116.9 30.1 %copy-start.5 = (bf16[256,256]{1,0:T(8,128)(2,1)S(1)}, bf16[256,256]{1,0:T(8,128)(2,1)}, u32[]{:S(2)}) copy-start(bf16[256,256]{1,0:T(8,128)(2,1)} %param.15) | copy-start | bytes 393220
  116.9 30.1 %copy-start.6 = (f32[256]{0:T(256)S(1)}, f32[256]{0:T(256)}, u32[]{:S(2)}) copy-start(f32[256]{0:T(256)} %param.14) | copy-start | bytes 3076
  120.4 1.2 copy-start.2
  121.6 127.1 %all-gather.7.cloned.1.call-start = ((), (), s32[]{:S(2)}) async-start(), calls=%async_computation.7 | async-start | bytes 1056768 | tf_op jit(solution)/shard_map/all_gather | solution.py:19
  158.2 90.5 %all-to-all-start.1 = ((bf16[128,16,256]{2,1,0:T(8,128)(2,1)}), bf16[128,16,256]{2,1,0:T(8,128)(2,1)S(1)}, u32[]{:S(2)}, u32[]{:S(2)}) async-start(bf16[128,16,256]{2,1,0:T(8,128)(2,1)} %broadcast_select_fusion), calls=%async_computation.2 | async-start | bytes 2097152 | tf_op jit(solution)/shard_map/all_to_all | solution.py:16
  173.5 113.4 %reduce-scatter.5.cloned.1.call-start = ((), (), s32[]{:S(2)}) async-start(), calls=%async_computation.5 | async-start | bytes 1966080 | tf_op jit(solution)/shard_map/reduce_scatter | solution.py:45
  248.7 1.0 copy-start.4
  256.7 30.1 %copy-start.7 = (f32[256]{0:T(256)S(1)}, f32[256]{0:T(256)}, u32[]{:S(2)}) copy-start(f32[256]{0:T(256)} %param.16) | copy-start | bytes 3076
  260.2 1.2 copy-start.1
Sparse Core Ops, SparseCore 0:
  10.4 98.4 all-gather.4
  121.7 25.2 reduce-scatter.2
  157.1 91.6 all-gather.6
  261.6 25.2 reduce-scatter.4
where the time goes:
time: 296 us; the launch traced here: 295 us
  waiting for transfers between devices  196 us (66%)
  starting transfers between devices  33.8 us (11%)
  local copies, waits for them, and re-layouts  29 us (10%)
  other arithmetic  16.8 us (6%)
  between operations  14 us (5%)
  matrix products  5.74 us (2%)
    all_gather x2, waiting for transfers between devices, collect(): hubs_in = lax.all_gather(hub_local, 'dom', axis=0, tiled=True)  145 us
    reduce_scatter x2, waiting for transfers between devices, aggregate(): lax.psum_scatter(partial_sums, 'cuts', scatter_dimension=0, tiled=True)  50.8 us
    all_to_all x2, starting transfers between devices, collect(): lax.all_to_all(outgoing, 'dom', split_axis=0, concat_axis=0, tiled=True)  33.7 us
    gather x2, local copies, waits for them, and re-layouts, collect(): table[picks]  15 us
    scatter-add x2, other arithmetic, group_sum(): return totals.at[targets].add(products)  7 us
  transfers between devices with their start and end apart: 6, of which 4 were waited for; matrix products, arithmetic and copies ran while one was open for 4% of the time, Pallas kernels for 0%

commit v1 on v0

v1 whole, which is shorter than its diff:
```python
import jax
import jax.numpy as jnp
from jax import lax
from jax.experimental import pallas as pl
from jax.experimental.pallas import tpu as pltpu
from jax.sharding import PartitionSpec as P

ROWS = 384
SLOT = 16
HUB = 16
BLOCK = 128
CHUNK = 16
VMEM = pltpu.VMEM
SMEM = pltpu.SMEM
F32 = jnp.float32
BF16 = jnp.bfloat16


def spec(space):
    return pl.BlockSpec(memory_space=space)


def call(body, out_shape, spaces, scratch=()):
    return pl.pallas_call(
        body,
        out_shape=out_shape,
        in_specs=[spec(s) for s in spaces],
        out_specs=jax.tree.map(lambda _: spec(VMEM), out_shape),
        scratch_shapes=list(scratch),
        compiler_params=pltpu.CompilerParams(vmem_limit_bytes=40 * 1024 * 1024),
    )


def column(row, size):
    here = lax.broadcasted_iota(jnp.int32, (size, size), 0)
    there = lax.broadcasted_iota(jnp.int32, (size, size), 1)
    return jnp.sum(jnp.where(here == there, row, 0), axis=1, keepdims=True)


def one_hot(picks, depth):
    places = lax.broadcasted_iota(jnp.int32, (picks.shape[0], depth), 1)
    return jnp.where(picks == places, 1.0, 0.0).astype(BF16)


def fill_outgoing(table, halo_rows, halo_count, hub_rows, out):
    parts, slots = halo_rows.shape
    counts = column(halo_count[...], parts)
    slot = lax.broadcasted_iota(jnp.int32, (parts, slots), 1)
    picks = jnp.where(slot < counts, halo_rows[...], -1)
    hubs = jnp.dot(
        one_hot(column(hub_rows[...], HUB), ROWS), table, preferred_element_type=F32
    ).astype(BF16)
    for first in range(0, parts, CHUNK):
        some = picks[first : first + CHUNK]
        wide = jnp.broadcast_to(some[:, :, None], (CHUNK, slots, ROWS)).reshape(
            CHUNK * slots, ROWS
        )
        places = lax.broadcasted_iota(jnp.int32, (CHUNK * slots, ROWS), 1)
        chosen = jnp.where(wide == places, 1.0, 0.0).astype(BF16)
        rows = jnp.dot(chosen, table, preferred_element_type=F32).astype(BF16)
        out[first : first + CHUNK, :slots] = rows.reshape(CHUNK, slots, -1)
        out[first : first + CHUNK, slots:] = jnp.broadcast_to(
            hubs[None], (CHUNK,) + hubs.shape
        )


def pack_body(table, halo_rows, halo_count, hub_rows, out):
    fill_outgoing(table[...], halo_rows, halo_count, hub_rows, out)


def pack(table, halo_rows, halo_count, hub_rows):
    parts = halo_rows.shape[0]
    return call(
        pack_body,
        jax.ShapeDtypeStruct((parts, SLOT + HUB, table.shape[1]), BF16),
        [VMEM] * 4,
    )(table, halo_rows, halo_count, hub_rows)


def sum_body(targets, sources, count, own, incoming, tiles, out, mine, total):
    total[...] = jnp.zeros_like(total)
    capacity = tiles.shape[0]
    group = BLOCK // SLOT
    groups = incoming.shape[0] // group
    own_blocks = ROWS // BLOCK
    width = own.shape[1]
    used = count[0]
    for i in range(capacity):
        col = sources[i]
        here = jnp.minimum(col, own_blocks - 1)
        local_rows = own[pl.ds(pl.multiple_of(here * BLOCK, BLOCK), BLOCK), :]
        away = jnp.maximum(col - own_blocks, 0)
        hub = jnp.where(away >= groups, 1, 0)
        first = pl.multiple_of((away - hub * groups) * group, group)
        remote_rows = incoming[
            pl.ds(first, group), pl.ds(pl.multiple_of(hub * SLOT, SLOT), SLOT), :
        ].reshape(BLOCK, width)
        rows = jnp.where(col < own_blocks, local_rows, remote_rows)
        term = jnp.dot(tiles[i], rows, preferred_element_type=F32)
        row = targets[i]
        total[row] = total[row] + jnp.where(i < used, term, 0.0)
    chunk = ROWS // BLOCK
    cut = lax.axis_index("cuts")
    mine[...] = total[pl.ds(cut * chunk, chunk)].reshape(ROWS, width)
    out[...] = total[...].astype(BF16).reshape(out.shape)


def tile_sums(own, incoming, tile_target, tile_source, tile_count, tiles, cuts):
    width = own.shape[1]
    return call(
        sum_body,
        (
            jax.ShapeDtypeStruct((cuts, ROWS, width), BF16),
            jax.ShapeDtypeStruct((ROWS, width), F32),
        ),
        [SMEM] * 3 + [VMEM] * 3,
        [pltpu.VMEM((cuts * ROWS // BLOCK, BLOCK, width), F32)],
    )(tile_target, tile_source, tile_count, own, incoming, tiles)


def over_cuts(parts, mine):
    cut = lax.axis_index("cuts")
    total = mine[...]
    for k in range(parts.shape[0]):
        total = total + jnp.where(cut == k, 0.0, parts[k].astype(F32))
    return total


def middle_body(
    parts, mine, w_one, b_one, w_two, halo_rows, halo_count, hub_rows, table, out
):
    total = over_cuts(parts, mine)
    high = total.astype(BF16)
    low = (total - high.astype(F32)).astype(BF16)
    hidden = jnp.dot(high, w_one[...], preferred_element_type=F32) + jnp.dot(
        low, w_one[...], preferred_element_type=F32
    )
    hidden = jnp.maximum(hidden + b_one[...], 0.0).astype(BF16)
    projected = jnp.dot(hidden, w_two[...], preferred_element_type=F32).astype(BF16)
    table[...] = projected
    fill_outgoing(projected, halo_rows, halo_count, hub_rows, out)


def middle(parts, mine, w_one, b_one, w_two, halo_rows, halo_count, hub_rows):
    width = w_two.shape[1]
    return call(
        middle_body,
        (
            jax.ShapeDtypeStruct((ROWS, width), BF16),
            jax.ShapeDtypeStruct((halo_rows.shape[0], SLOT + HUB, width), BF16),
        ),
        [VMEM] * 8,
    )(parts, mine, w_one, b_one, w_two, halo_rows, halo_count, hub_rows)


def last_body(parts, mine, bias, out):
    out[...] = jnp.maximum(over_cuts(parts, mine) + bias[...], 0.0).astype(BF16)


def swap(rows, axis):
    return lax.all_to_all(rows, axis, split_axis=0, concat_axis=0, tiled=True)


def local(
    features,
    weight_one,
    bias_one,
    weight_two,
    bias_two,
    hub_rows,
    halo_rows,
    halo_count,
    tile_target,
    tile_source,
    tile_count,
    tile_values,
):
    cuts = lax.axis_size("cuts")
    halo_rows = halo_rows.reshape(halo_rows.shape[2:])
    halo_count = halo_count.reshape(1, -1)
    hub_rows = hub_rows.reshape(1, -1)
    tiles = tile_values.reshape(tile_values.shape[2:])
    plan = (tile_target.reshape(-1), tile_source.reshape(-1), tile_count.reshape(-1))

    incoming = swap(pack(features, halo_rows, halo_count, hub_rows), "dom")
    parts, mine = tile_sums(features, incoming, *plan, tiles, cuts)
    table, outgoing = middle(
        swap(parts, "cuts"),
        mine,
        weight_one,
        bias_one.reshape(1, -1),
        weight_two,
        halo_rows,
        halo_count,
        hub_rows,
    )
    incoming = swap(outgoing, "dom")
    parts, mine = tile_sums(table, incoming, *plan, tiles, cuts)
    return call(
        last_body, jax.ShapeDtypeStruct(table.shape, BF16), [VMEM] * 3
    )(swap(parts, "cuts"), mine, bias_two.reshape(1, -1))


def solution(mesh):
    return jax.shard_map(
        local,
        mesh=mesh,
        in_specs=(
            P(("dom", "cuts"), None),
            P(),
            P(),
            P(),
            P(),
            P("dom", "cuts", None),
            P("dom", "cuts", None, None),
            P("dom", "cuts", None),
            P("dom", "cuts", None),
            P("dom", "cuts", None),
            P("dom", "cuts"),
            P("dom", "cuts", None, None, None),
        ),
        out_specs=P(("dom", "cuts"), None),
        check_vma=False,
    )
```

time: 296 us -> 144 us (0.49)
  waiting for transfers between devices: 196 us -> 29.8 us
  blocking collectives: 0 us -> 84.9 us
  local copies, waits for them, and re-layouts: 29 us -> 3.09 us
  other arithmetic: 16.8 us -> 0 us
  starting transfers between devices: 33.8 us -> 18.6 us
  between operations: 14 us -> 0.74 us
  Pallas kernels: 0 us -> 6.5 us
  matrix products: 5.74 us -> 0 us
    all_gather x2 -> x0, waiting for transfers between devices: 145 us -> none  [collect(): hubs_in = lax.all_gather(hub_local, 'dom', axis=0, tiled=True)]
    all_to_all x0 -> x3, blocking collectives: none -> 84.9 us  [swap(): return lax.all_to_all(rows, axis, split_axis=0, concat_axis=0, tiled=True)]
    reduce_scatter x2 -> x0, waiting for transfers between devices: 50.8 us -> none  [aggregate(): lax.psum_scatter(partial_sums, 'cuts', scatter_dimension=0, tiled=True)]
    all_to_all x2 -> x1, waiting for transfers between devices: 0.01 us -> 29.8 us  [swap(): return lax.all_to_all(rows, axis, split_axis=0, concat_axis=0, tiled=True)]
    gather x6 -> x0, local copies, waits for them, and re-layouts: 20.6 us -> none  [the longest x2 15 us: collect(): table[picks]]
    all_to_all x2 -> x1, starting transfers between devices: 33.7 us -> 18.6 us  [swap(): return lax.all_to_all(rows, axis, split_axis=0, concat_axis=0, tiled=True)]
    scatter-add x2 -> x0, other arithmetic: 7 us -> none  [group_sum(): return totals.at[targets].add(products)]
    pallas_call x0 -> x5, Pallas kernels: none -> 6.5 us  [the longest x2 2.16 us: tile_sums(): call(sum_body, (jax.ShapeDtypeStruct((cuts, ROWS, width), BF16), jax.Shap...]
  transfers between devices with their start and end apart: 6 -> 1, of which waited for: 4 -> 1; matrix products, arithmetic and copies ran while one was open for 4% -> 0% of each run, Pallas kernels for 0% -> 0%
where the time goes in v1:
time: 144 us
  blocking collectives  84.9 us (59%)
  waiting for transfers between devices  29.8 us (21%)
  starting transfers between devices  18.6 us (13%)
  Pallas kernels  6.5 us (5%)
  local copies, waits for them, and re-layouts  3.09 us (2%)
    all_to_all x3, blocking collectives, swap(): return lax.all_to_all(rows, axis, split_axis=0, concat_axis=0, tiled=True)  84.9 us
    all_to_all x1, waiting for transfers between devices, swap(): return lax.all_to_all(rows, axis, split_axis=0, concat_axis=0, tiled=True)  29.8 us
    all_to_all x1, starting transfers between devices, swap(): return lax.all_to_all(rows, axis, split_axis=0, concat_axis=0, tiled=True)  18.6 us
    unnamed x27, local copies, waits for them, and re-layouts  3.09 us
  transfers between devices with their start and end apart: 1, of which 1 were waited for; matrix products, arithmetic and copies ran while one was open for 0% of the time, Pallas kernels for 0%

profile of v1, /device:TPU:1, one launch (start us, length us, event | category | flops | bytes accessed | tf_op | source)
XLA Modules:
  0.0 143.6 jit_solution(8931059137111322446)
XLA Ops:
  0.0 0.9 copy.13
  0.9 0.9 copy-done.1
  1.8 0.7 copy-done.5
  2.4 0.7 copy-done.7
  3.1 2.1 %shard_map.118 = bf16[128,32,128]{2,1,0:T(8,128)(2,1)} custom-call(bf16[384,128]{1,0:T(8,128)(2,1)S(1)} %copy-done.1, s32[128,16]{1,0:T(8,128)S(1)} %bitcast.13, s32[1,128]{1,0:T(1,128)S(1)} %bitcast.15, s32[1,16]{1,0:T(1,128)S(1)} %bitcast.17), custom_call_target="tpu_custom_call" | custom-call | tf_op jit(solution)/shard_map/pallas_call | solution.py:73
  5.2 0.0 copy-start.11
  5.2 18.6 %all-to-all-start = ((bf16[128,32,128]{2,1,0:T(8,128)(2,1)}), bf16[128,32,128]{2,1,0:T(8,128)(2,1)S(1)}, u32[]{:S(2)}, u32[]{:S(2)}) async-start(bf16[128,32,128]{2,1,0:T(8,128)(2,1)} %shard_map.118), calls=%async_computation | async-start | bytes 2097152 | tf_op jit(solution)/shard_map/all_to_all | solution.py:161
  24.4 29.8 %all-to-all-done.incoming = bf16[128,32,128]{2,1,0:T(8,128)(2,1)S(1)} async-done(((bf16[128,32,128]{2,1,0:T(8,128)(2,1)}), bf16[128,32,128]{2,1,0:T(8,128)(2,1)S(1)}, u32[]{:S(2)}, u32[]{:S(2)}) %all-to-all-start) | async-done | bytes 1048608 | tf_op jit(solution)/shard_map/all_to_all | solution.py:161
  54.2 0.0 copy-done
  54.2 0.0 copy-done.2
  54.2 0.0 copy-done.9
  54.2 0.0 copy-done.10
  54.2 1.0 shard_map.119
  55.2 10.1 %all_to_all.20.parts = bf16[4,384,128]{2,1,0:T(8,128)(2,1)S(1)} all-to-all(bf16[4,384,128]{2,1,0:T(8,128)(2,1)S(1)} %get-tuple-element.11), channel_id=1, replica_groups=mesh['dom'=128,'cuts'=4] {'cuts'}, dimensions={0} | all-to-all | bytes 786432 | tf_op jit(solution)/shard_map/all_to_all | solution.py:161
  65.3 0.0 copy-done.3
  65.3 0.0 copy-done.4
  65.3 0.0 copy-done.6
  65.3 0.0 copy-done.8
  65.3 0.0 copy-done.11
  65.3 1.3 shard_map.120
  66.7 61.0 %all_to_all.21.incoming = bf16[128,32,256]{2,1,0:T(8,128)(2,1)S(1)} all-to-all(bf16[128,32,256]{2,1,0:T(8,128)(2,1)S(1)} %get-tuple-element.14), channel_id=1, replica_groups=mesh['dom'=128,'cuts'=4] {'dom'}, dimensions={0} | all-to-all | bytes 4194304 | tf_op jit(solution)/shard_map/all_to_all | solution.py:161
  127.7 1.2 shard_map.121
  128.9 13.8 %all_to_all.22.parts = bf16[4,384,256]{2,1,0:T(8,128)(2,1)S(1)} all-to-all(bf16[4,384,256]{2,1,0:T(8,128)(2,1)S(1)} %get-tuple-element.15), channel_id=1, replica_groups=mesh['dom'=128,'cuts'=4] {'cuts'}, dimensions={0} | all-to-all | bytes 1572864 | tf_op jit(solution)/shard_map/all_to_all | solution.py:161
  142.7 0.9 shard_map.122
  (13 shorter events, 0.0 us)
Async XLA Ops:
  0.0 54.2 %copy-start = (bf16[1,1,16,128,128]{4,3,2,1,0:T(8,128)(2,1)S(1)}, bf16[1,1,16,128,128]{4,3,2,1,0:T(8,128)(2,1)}, u32[]{:S(2)}) copy-start(bf16[1,1,16,128,128]{4,3,2,1,0:T(8,128)(2,1)} %param.23) | copy-start | bytes 1572868
  0.9 0.9 copy-start.1
  1.8 0.7 copy-start.5
  2.4 0.7 copy-start.7
  3.1 51.2 %copy-start.2 = (bf16[384,128]{1,0:T(8,128)(2,1)S(1)}, bf16[384,128]{1,0:T(8,128)(2,1)}, u32[]{:S(2)}) copy-start(bf16[384,128]{1,0:T(8,128)(2,1)} %own.1) | copy-start | bytes 294916
  3.1 51.2 %copy-start.9 = (s32[1,1,16]{2,1,0:T(1,128)S(1)}, s32[1,1,16]{2,1,0:T(1,128)}, u32[]{:S(2)}) copy-start(s32[1,1,16]{2,1,0:T(1,128)} %param.20) | copy-start | bytes 196
  3.1 51.2 %copy-start.10 = (s32[1,1,16]{2,1,0:T(1,128)S(1)}, s32[1,1,16]{2,1,0:T(1,128)}, u32[]{:S(2)}) copy-start(s32[1,1,16]{2,1,0:T(1,128)} %param.21) | copy-start | bytes 196
  5.2 60.1 %copy-start.3 = (bf16[256,256]{1,0:T(8,128)(2,1)S(1)}, bf16[256,256]{1,0:T(8,128)(2,1)}, u32[]{:S(2)}) copy-start(bf16[256,256]{1,0:T(8,128)(2,1)} %w_two.1) | copy-start | bytes 393220
  5.2 60.1 %copy-start.4 = (bf16[128,256]{1,0:T(8,128)(2,1)S(1)}, bf16[128,256]{1,0:T(8,128)(2,1)}, u32[]{:S(2)}) copy-start(bf16[128,256]{1,0:T(8,128)(2,1)} %w_one.1) | copy-start | bytes 196612
  5.2 60.1 %copy-start.6 = (s32[1,1,128]{2,1,0:T(1,128)S(1)}, s32[1,1,128]{2,1,0:T(1,128)}, u32[]{:S(2)}) copy-start(s32[1,1,128]{2,1,0:T(1,128)} %param.19) | copy-start | bytes 1540
  5.2 60.1 %copy-start.8 = (s32[1,1,16]{2,1,0:T(1,128)S(1)}, s32[1,1,16]{2,1,0:T(1,128)}, u32[]{:S(2)}) copy-start(s32[1,1,16]{2,1,0:T(1,128)} %param.17) | copy-start | bytes 196
  5.2 60.1 %copy-start.11 = (f32[256]{0:T(256)S(1)}, f32[256]{0:T(256)}, u32[]{:S(2)}) copy-start(f32[256]{0:T(256)} %param.14) | copy-start | bytes 3076
  5.2 49.0 %all-to-all-start = ((bf16[128,32,128]{2,1,0:T(8,128)(2,1)}), bf16[128,32,128]{2,1,0:T(8,128)(2,1)S(1)}, u32[]{:S(2)}, u32[]{:S(2)}) async-start(bf16[128,32,128]{2,1,0:T(8,128)(2,1)} %shard_map.118), calls=%async_computation | async-start | bytes 2097152 | tf_op jit(solution)/shard_map/all_to_all | solution.py:161
  127.7 15.0 %copy-start.12 = (f32[256]{0:T(256)S(1)}, f32[256]{0:T(256)}, u32[]{:S(2)}) copy-start(f32[256]{0:T(256)} %param.16) | copy-start | bytes 3076

commit v2 on v1

--- a/solution.py
+++ b/solution.py
@@ -10,6 +10,8 @@
 HUB = 16
 BLOCK = 128
 CHUNK = 16
+DEAD = 2.0**100
+DEAD_LIMIT = 2.0**50
 VMEM = pltpu.VMEM
 SMEM = pltpu.SMEM
 F32 = jnp.float32
@@ -42,8 +44,9 @@
     return jnp.where(picks == places, 1.0, 0.0).astype(BF16)
 
 
-def fill_outgoing(table, halo_rows, halo_count, hub_rows, out):
+def fill_outgoing(table, halo_rows, halo_count, hub_rows, out, dead):
     parts, slots = halo_rows.shape
+    width = table.shape[1]
     counts = column(halo_count[...], parts)
     slot = lax.broadcasted_iota(jnp.int32, (parts, slots), 1)
     picks = jnp.where(slot < counts, halo_rows[...], -1)
@@ -57,15 +60,19 @@
         )
         places = lax.broadcasted_iota(jnp.int32, (CHUNK * slots, ROWS), 1)
         chosen = jnp.where(wide == places, 1.0, 0.0).astype(BF16)
-        rows = jnp.dot(chosen, table, preferred_element_type=F32).astype(BF16)
-        out[first : first + CHUNK, :slots] = rows.reshape(CHUNK, slots, -1)
+        rows = jnp.dot(chosen, table, preferred_element_type=F32)
+        if dead != 0.0:
+            rows = jnp.where(wide[:, :width] < 0, dead, rows)
+        out[first : first + CHUNK, :slots] = rows.astype(BF16).reshape(
+            CHUNK, slots, width
+        )
         out[first : first + CHUNK, slots:] = jnp.broadcast_to(
             hubs[None], (CHUNK,) + hubs.shape
         )
 
 
 def pack_body(table, halo_rows, halo_count, hub_rows, out):
-    fill_outgoing(table[...], halo_rows, halo_count, hub_rows, out)
+    fill_outgoing(table[...], halo_rows, halo_count, hub_rows, out, 0.0)
 
 
 def pack(table, halo_rows, halo_count, hub_rows):
@@ -77,13 +84,13 @@
     )(table, halo_rows, halo_count, hub_rows)
 
 
-def sum_body(targets, sources, count, own, incoming, tiles, out, mine, total):
+def sum_body(targets, sources, count, own, incoming, tiles, *rest):
+    *layer, out, mine, total = rest
     total[...] = jnp.zeros_like(total)
     capacity = tiles.shape[0]
     group = BLOCK // SLOT
     groups = incoming.shape[0] // group
     own_blocks = ROWS // BLOCK
-    width = own.shape[1]
     used = count[0]
     for i in range(capacity):
         col = sources[i]
@@ -94,28 +101,35 @@
         first = pl.multiple_of((away - hub * groups) * group, group)
         remote_rows = incoming[
             pl.ds(first, group), pl.ds(pl.multiple_of(hub * SLOT, SLOT), SLOT), :
-        ].reshape(BLOCK, width)
+        ].reshape(BLOCK, own.shape[1])
         rows = jnp.where(col < own_blocks, local_rows, remote_rows)
+        if layer:
+            weight, bias = layer
+            hidden = jnp.dot(rows, weight[...], preferred_element_type=F32)
+            hidden = jnp.maximum(hidden + bias[...], 0.0)
+            live = rows.astype(F32) < DEAD_LIMIT
+            live = jnp.concatenate([live] * (hidden.shape[1] // live.shape[1]), axis=1)
+            rows = jnp.where(live, hidden, 0.0).astype(BF16)
         term = jnp.dot(tiles[i], rows, preferred_element_type=F32)
         row = targets[i]
         total[row] = total[row] + jnp.where(i < used, term, 0.0)
     chunk = ROWS // BLOCK
     cut = lax.axis_index("cuts")
-    mine[...] = total[pl.ds(cut * chunk, chunk)].reshape(ROWS, width)
+    mine[...] = total[pl.ds(cut * chunk, chunk)].reshape(mine.shape)
     out[...] = total[...].astype(BF16).reshape(out.shape)
 
 
-def tile_sums(own, incoming, tile_target, tile_source, tile_count, tiles, cuts):
-    width = own.shape[1]
+def tile_sums(own, incoming, tile_target, tile_source, tile_count, tiles, cuts, *layer):
+    width = layer[0].shape[1] if layer else own.shape[1]
     return call(
         sum_body,
         (
             jax.ShapeDtypeStruct((cuts, ROWS, width), BF16),
             jax.ShapeDtypeStruct((ROWS, width), F32),
         ),
-        [SMEM] * 3 + [VMEM] * 3,
+        [SMEM] * 3 + [VMEM] * (3 + len(layer)),
         [pltpu.VMEM((cuts * ROWS // BLOCK, BLOCK, width), F32)],
-    )(tile_target, tile_source, tile_count, own, incoming, tiles)
+    )(tile_target, tile_source, tile_count, own, incoming, tiles, *layer)
 
 
 def over_cuts(parts, mine):
@@ -126,35 +140,32 @@
     return total
 
 
-def middle_body(
-    parts, mine, w_one, b_one, w_two, halo_rows, halo_count, hub_rows, table, out
-):
-    total = over_cuts(parts, mine)
-    high = total.astype(BF16)
-    low = (total - high.astype(F32)).astype(BF16)
-    hidden = jnp.dot(high, w_one[...], preferred_element_type=F32) + jnp.dot(
-        low, w_one[...], preferred_element_type=F32
-    )
-    hidden = jnp.maximum(hidden + b_one[...], 0.0).astype(BF16)
-    projected = jnp.dot(hidden, w_two[...], preferred_element_type=F32).astype(BF16)
-    table[...] = projected
-    fill_outgoing(projected, halo_rows, halo_count, hub_rows, out)
-
-
-def middle(parts, mine, w_one, b_one, w_two, halo_rows, halo_count, hub_rows):
-    width = w_two.shape[1]
+def middle_body(parts, mine, halo_rows, halo_count, hub_rows, table, out):
+    rows = over_cuts(parts, mine).astype(BF16)
+    table[...] = rows
+    fill_outgoing(rows, halo_rows, halo_count, hub_rows, out, DEAD)
+
+
+def middle(parts, mine, halo_rows, halo_count, hub_rows):
+    width = mine.shape[1]
     return call(
         middle_body,
         (
             jax.ShapeDtypeStruct((ROWS, width), BF16),
             jax.ShapeDtypeStruct((halo_rows.shape[0], SLOT + HUB, width), BF16),
         ),
-        [VMEM] * 8,
-    )(parts, mine, w_one, b_one, w_two, halo_rows, halo_count, hub_rows)
-
-
-def last_body(parts, mine, bias, out):
-    out[...] = jnp.maximum(over_cuts(parts, mine) + bias[...], 0.0).astype(BF16)
+        [VMEM] * 5,
+    )(parts, mine, halo_rows, halo_count, hub_rows)
+
+
+def last_body(parts, mine, weight, bias, out):
+    total = over_cuts(parts, mine)
+    high = total.astype(BF16)
+    low = (total - high.astype(F32)).astype(BF16)
+    hidden = jnp.dot(high, weight[...], preferred_element_type=F32) + jnp.dot(
+        low, weight[...], preferred_element_type=F32
+    )
+    out[...] = jnp.maximum(hidden + bias[...], 0.0).astype(BF16)
 
 
 def swap(rows, axis):
@@ -185,20 +196,17 @@
     incoming = swap(pack(features, halo_rows, halo_count, hub_rows), "dom")
     parts, mine = tile_sums(features, incoming, *plan, tiles, cuts)
     table, outgoing = middle(
-        swap(parts, "cuts"),
-        mine,
-        weight_one,
-        bias_one.reshape(1, -1),
-        weight_two,
-        halo_rows,
-        halo_count,
-        hub_rows,
+        swap(parts, "cuts"), mine, halo_rows, halo_count, hub_rows
     )
     incoming = swap(outgoing, "dom")
-    parts, mine = tile_sums(table, incoming, *plan, tiles, cuts)
-    return call(
-        last_body, jax.ShapeDtypeStruct(table.shape, BF16), [VMEM] * 3
-    )(swap(parts, "cuts"), mine, bias_two.reshape(1, -1))
+    parts, mine = tile_sums(
+        table, incoming, *plan, tiles, cuts, weight_one, bias_one.reshape(1, -1)
+    )
+    return call(
+        last_body,
+        jax.ShapeDtypeStruct((ROWS, weight_two.shape[1]), BF16),
+        [VMEM] * 4,
+    )(swap(parts, "cuts"), mine, weight_two, bias_two.reshape(1, -1))
 
 
 def solution(mesh):

time: 144 us -> 124 us (0.86)
  blocking collectives: 84.9 us -> 62.8 us
    all_to_all x3, blocking collectives: 84.9 us -> 62.8 us  [swap(): return lax.all_to_all(rows, axis, split_axis=0, concat_axis=0, tiled=True)]
    unnamed x27 -> x23, local copies, waits for them, and re-layouts: 3.09 us -> 4.38 us
where the time goes in v2:
time: 124 us; the launch traced here: 123 us
  blocking collectives  62.8 us (51%)
  waiting for transfers between devices  29.8 us (24%)
  starting transfers between devices  18.5 us (15%)
  Pallas kernels  6.85 us (6%)
  local copies, waits for them, and re-layouts  4.38 us (4%)
    all_to_all x3, blocking collectives, swap(): return lax.all_to_all(rows, axis, split_axis=0, concat_axis=0, tiled=True)  62.8 us
    all_to_all x1, waiting for transfers between devices, swap(): return lax.all_to_all(rows, axis, split_axis=0, concat_axis=0, tiled=True)  29.8 us
    all_to_all x1, starting transfers between devices, swap(): return lax.all_to_all(rows, axis, split_axis=0, concat_axis=0, tiled=True)  18.5 us
    unnamed x23, local copies, waits for them, and re-layouts  4.38 us
    pallas_call x2, Pallas kernels, tile_sums(): call(sum_body, (jax.ShapeDtypeStruct((cuts, ROWS, width), BF16), jax.Shap...  2.59 us
  transfers between devices with their start and end apart: 1, of which 1 were waited for; matrix products, arithmetic and copies ran while one was open for 0% of the time, Pallas kernels for 0%

profile of v2, /device:TPU:1, one launch (start us, length us, event | category | flops | bytes accessed | tf_op | source)
XLA Modules:
  0.0 123.1 jit_solution(15877377242297226622)
XLA Ops:
  0.0 0.8 copy.13
  0.8 0.0 copy-start.8
  0.8 0.6 copy-done.7
  1.5 0.0 copy-done.8
  1.5 0.9 copy-done.1
  2.4 2.1 %shard_map.118 = bf16[128,32,128]{2,1,0:T(8,128)(2,1)} custom-call(bf16[384,128]{1,0:T(8,128)(2,1)S(1)} %copy-done.1, s32[128,16]{1,0:T(8,128)S(1)} %bitcast.13, s32[1,128]{1,0:T(1,128)S(1)} %bitcast.19, s32[1,16]{1,0:T(1,128)S(1)} %bitcast.21), custom_call_target="tpu_custom_call" | custom-call | tf_op jit(solution)/shard_map/pallas_call | solution.py:80
  4.5 18.5 %all-to-all-start = ((bf16[128,32,128]{2,1,0:T(8,128)(2,1)}), bf16[128,32,128]{2,1,0:T(8,128)(2,1)S(1)}, u32[]{:S(2)}, u32[]{:S(2)}) async-start(bf16[128,32,128]{2,1,0:T(8,128)(2,1)} %shard_map.118), calls=%async_computation | async-start | bytes 2097152 | tf_op jit(solution)/shard_map/all_to_all | solution.py:172
  23.7 29.8 %all-to-all-done.incoming = bf16[128,32,128]{2,1,0:T(8,128)(2,1)S(1)} async-done(((bf16[128,32,128]{2,1,0:T(8,128)(2,1)}), bf16[128,32,128]{2,1,0:T(8,128)(2,1)S(1)}, u32[]{:S(2)}, u32[]{:S(2)}) %all-to-all-start) | async-done | bytes 1048608 | tf_op jit(solution)/shard_map/all_to_all | solution.py:172
  53.5 0.0 copy-done
  53.5 0.0 copy-done.2
  53.5 0.6 copy-done.5
  54.1 0.0 copy-done.6
  54.1 1.0 shard_map.119
  55.1 10.1 %all_to_all.20.parts = bf16[4,384,128]{2,1,0:T(8,128)(2,1)S(1)} all-to-all(bf16[4,384,128]{2,1,0:T(8,128)(2,1)S(1)} %get-tuple-element.11), channel_id=1, replica_groups=mesh['dom'=128,'cuts'=4] {'cuts'}, dimensions={0} | all-to-all | bytes 786432 | tf_op jit(solution)/shard_map/all_to_all | solution.py:172
  65.2 1.1 shard_map.120
  66.3 0.0 copy-start.4
  66.3 39.5 %all_to_all.21.incoming = bf16[128,32,128]{2,1,0:T(8,128)(2,1)S(1)} all-to-all(bf16[128,32,128]{2,1,0:T(8,128)(2,1)S(1)} %get-tuple-element.14), channel_id=1, replica_groups=mesh['dom'=128,'cuts'=4] {'dom'}, dimensions={0} | all-to-all | bytes 2097152 | tf_op jit(solution)/shard_map/all_to_all | solution.py:172
  105.8 0.0 copy-done.4
  105.8 0.7 copy-done.9
  106.5 1.6 %shard_map.121 = (bf16[4,384,256]{2,1,0:T(8,128)(2,1)S(1)}, f32[384,256]{1,0:T(8,128)S(1)}) custom-call(s32[16]{0:T(128)S(1)} %bitcast.16, s32[16]{0:T(128)S(1)} %bitcast.18, s32[1]{0:T(128)} %bitcast.10.count, bf16[384,128]{1,0:T(8,128)(2,1)S(1)} %get-tuple-element.13.own, bf16[128,32,128]{2,1,0:T(8,128)(2,1)S(1)} %all_to_all.21.incoming, ...), custom_call_target="tpu_custom_call" | custom-call | tf_op jit(solution)/shard_map/pallas_call | solution.py:124
  108.1 0.0 copy-start.3
  108.1 13.2 %all_to_all.22.parts = bf16[4,384,256]{2,1,0:T(8,128)(2,1)S(1)} all-to-all(bf16[4,384,256]{2,1,0:T(8,128)(2,1)S(1)} %get-tuple-element.15), channel_id=1, replica_groups=mesh['dom'=128,'cuts'=4] {'cuts'}, dimensions={0} | all-to-all | bytes 1572864 | tf_op jit(solution)/shard_map/all_to_all | solution.py:172
  121.4 0.7 copy-done.10
  122.0 1.0 shard_map.122
  (9 shorter events, 0.0 us)
Async XLA Ops:
  0.8 0.7 copy-start.7
  0.8 0.7 copy-start.8
  1.5 0.9 copy-start.1
  4.5 49.0 %copy-start = (bf16[1,1,16,128,128]{4,3,2,1,0:T(8,128)(2,1)S(1)}, bf16[1,1,16,128,128]{4,3,2,1,0:T(8,128)(2,1)}, u32[]{:S(2)}) copy-start(bf16[1,1,16,128,128]{4,3,2,1,0:T(8,128)(2,1)} %param.23) | copy-start | bytes 1572868
  4.5 49.0 %copy-start.2 = (bf16[384,128]{1,0:T(8,128)(2,1)S(1)}, bf16[384,128]{1,0:T(8,128)(2,1)}, u32[]{:S(2)}) copy-start(bf16[384,128]{1,0:T(8,128)(2,1)} %own.1) | copy-start | bytes 294916
  4.5 49.0 %all-to-all-start = ((bf16[128,32,128]{2,1,0:T(8,128)(2,1)}), bf16[128,32,128]{2,1,0:T(8,128)(2,1)S(1)}, u32[]{:S(2)}, u32[]{:S(2)}) async-start(bf16[128,32,128]{2,1,0:T(8,128)(2,1)} %shard_map.118), calls=%async_computation | async-start | bytes 2097152 | tf_op jit(solution)/shard_map/all_to_all | solution.py:172
  53.5 0.7 copy-start.5
  53.5 0.7 copy-start.6
  66.3 39.5 %copy-start.4 = (bf16[128,256]{1,0:T(8,128)(2,1)S(1)}, bf16[128,256]{1,0:T(8,128)(2,1)}, u32[]{:S(2)}) copy-start(bf16[128,256]{1,0:T(8,128)(2,1)} %rest_0_.1) | copy-start | bytes 196612
  105.8 0.7 copy-start.9
  108.1 13.3 %copy-start.3 = (bf16[256,256]{1,0:T(8,128)(2,1)S(1)}, bf16[256,256]{1,0:T(8,128)(2,1)}, u32[]{:S(2)}) copy-start(bf16[256,256]{1,0:T(8,128)(2,1)} %weight.1) | copy-start | bytes 393220
  121.4 0.7 copy-start.10

commit v3 on v2

v3 whole, which is shorter than its diff:
```python
import jax
import jax.numpy as jnp
from jax import lax
from jax.experimental import pallas as pl
from jax.experimental.pallas import tpu as pltpu
from jax.sharding import PartitionSpec as P

ROWS = 384
SLOT = 16
HUB = 16
BLOCK = 128
CHUNK = 16
CORES = 2
DEAD = 2.0**100
DEAD_LIMIT = 2.0**50
VMEM = pltpu.VMEM
SMEM = pltpu.SMEM
F32 = jnp.float32
BF16 = jnp.bfloat16


def spec(space):
    return pl.BlockSpec(memory_space=space)


LIMIT = 40 * 1024 * 1024


def call(body, out_shape, spaces, scratch=()):
    return pl.pallas_call(
        body,
        out_shape=out_shape,
        in_specs=[spec(s) for s in spaces],
        out_specs=jax.tree.map(lambda _: spec(VMEM), out_shape),
        scratch_shapes=list(scratch),
        compiler_params=pltpu.CompilerParams(vmem_limit_bytes=LIMIT),
    )


def column(row, size):
    here = lax.broadcasted_iota(jnp.int32, (size, size), 0)
    there = lax.broadcasted_iota(jnp.int32, (size, size), 1)
    return jnp.sum(jnp.where(here == there, row, 0), axis=1, keepdims=True)


def one_hot(picks):
    places = lax.broadcasted_iota(jnp.int32, picks.shape, 1)
    return jnp.where(picks == places, 1.0, 0.0).astype(BF16)


def fill_outgoing(table, picks, hub_picks, out, dead):
    parts, slots = picks.shape
    width = table.shape[1]
    hubs = jnp.dot(one_hot(hub_picks), table, preferred_element_type=F32).astype(BF16)
    for first in range(0, parts, CHUNK):
        some = picks[first : first + CHUNK]
        wide = jnp.broadcast_to(some[:, :, None], (CHUNK, slots, ROWS)).reshape(
            CHUNK * slots, ROWS
        )
        rows = jnp.dot(one_hot(wide), table, preferred_element_type=F32)
        if dead != 0.0:
            rows = jnp.where(wide[:, :width] < 0, dead, rows)
        chips = pl.ds(first // CORES, CHUNK // CORES)
        out[chips, : CORES * slots] = rows.astype(BF16).reshape(
            CHUNK // CORES, CORES * slots, width
        )
        out[chips, CORES * slots :] = jnp.broadcast_to(
            hubs[None], (CHUNK // CORES,) + hubs.shape
        )


def pack_body(*refs):
    count = (len(refs) - 5) // 2
    sources, (out, picks_out, hubs_out, plan_out) = refs[:count], refs[count : count + 4]
    kept, sems = refs[count + 4 : -1], refs[-1]
    copies = [
        pltpu.make_async_copy(source, place, sems.at[i])
        for i, (source, place) in enumerate(zip(sources, kept, strict=True))
    ]
    for copy in copies:
        copy.start()
    for copy in copies:
        copy.wait()
    targets, columns, used, halo_rows, halo_count, hub_rows, table = kept[-7:]
    pieces = [targets[...], columns[...], used[...]]
    spare = plan_out.shape[1] - sum(piece.shape[1] for piece in pieces)
    plan_out[...] = jnp.concatenate(
        [*pieces, jnp.zeros((1, spare), jnp.int32)], axis=1
    )
    slots, parts = halo_rows.shape
    slot = lax.broadcasted_iota(jnp.int32, (slots, parts), 0)
    picks = jnp.where(slot < halo_count[...], halo_rows[...], -1).T
    hub_picks = jnp.broadcast_to(column(hub_rows[...], HUB), (HUB, ROWS))
    picks_out[...] = picks
    hubs_out[...] = hub_picks
    fill_outgoing(table[...], picks, hub_picks, out, 0.0)


def pack(handed, *operands):
    slots, parts = operands[-4].shape
    table = operands[-1]
    return pl.pallas_call(
        pack_body,
        out_shape=(
            jax.ShapeDtypeStruct((parts // CORES, CORES * SLOT + HUB, table.shape[1]), BF16),
            jax.ShapeDtypeStruct((parts, slots), jnp.int32),
            jax.ShapeDtypeStruct((HUB, ROWS), jnp.int32),
            jax.ShapeDtypeStruct((1, 128), jnp.int32),
            *(jax.ShapeDtypeStruct(x.shape, x.dtype) for x in handed),
        ),
        in_specs=[spec(pltpu.HBM)] * (len(handed) + len(operands)),
        out_specs=(spec(VMEM),) * (4 + len(handed)),
        scratch_shapes=[
            *(pltpu.VMEM(x.shape, x.dtype) for x in operands),
            pltpu.SemaphoreType.DMA((len(handed) + len(operands),)),
        ],
        compiler_params=pltpu.CompilerParams(vmem_limit_bytes=LIMIT),
    )(*handed, *operands)


def sum_body(plan, own, received, passed, tiles, *rest):
    *layer, out, mine, total = rest
    total[...] = jnp.zeros_like(total)
    capacity = tiles.shape[0]
    group = BLOCK // (CORES * SLOT)
    groups = received.shape[0] // group
    core = lax.rem(lax.axis_index("dom"), CORES)
    own_blocks = ROWS // BLOCK
    used = plan[2 * capacity]
    for i in range(capacity):
        col = plan[capacity + i]
        here = jnp.minimum(col, own_blocks - 1)
        local_rows = own[pl.ds(pl.multiple_of(here * BLOCK, BLOCK), BLOCK), :]
        away = jnp.maximum(col - own_blocks, 0)
        hub = jnp.where(away >= groups, 1, 0)
        first = pl.multiple_of((away - hub * groups) * group, group)
        start = pl.multiple_of(jnp.where(hub == 1, CORES * SLOT, core * SLOT), SLOT)
        same = received[pl.ds(first, group), pl.ds(start, SLOT), :]
        other = passed[pl.ds(first, group), pl.ds(start, SLOT), :]
        remote_rows = jnp.stack(
            [jnp.where(core == 0, same, other), jnp.where(core == 0, other, same)],
            axis=1,
        ).reshape(BLOCK, own.shape[1])
        rows = jnp.where(col < own_blocks, local_rows, remote_rows)
        if layer:
            weight, bias = layer
            hidden = jnp.dot(rows, weight[...], preferred_element_type=F32)
            hidden = jnp.maximum(hidden + bias[...], 0.0)
            live = rows.astype(F32) < DEAD_LIMIT
            live = jnp.concatenate([live] * (hidden.shape[1] // live.shape[1]), axis=1)
            rows = jnp.where(live, hidden, 0.0).astype(BF16)
        term = jnp.dot(tiles[i], rows, preferred_element_type=F32)
        row = plan[i]
        total[row] = total[row] + jnp.where(i < used, term, 0.0)
    chunk = ROWS // BLOCK
    cut = lax.axis_index("cuts")
    mine[...] = total[pl.ds(cut * chunk, chunk)].reshape(mine.shape)
    out[...] = total[...].astype(BF16).reshape(out.shape)


def tile_sums(own, received, passed, plan, tiles, cuts, *layer):
    width = layer[0].shape[1] if layer else own.shape[1]
    return call(
        sum_body,
        (
            jax.ShapeDtypeStruct((cuts, ROWS, width), BF16),
            jax.ShapeDtypeStruct((ROWS, width), F32),
        ),
        [SMEM] + [VMEM] * (4 + len(layer)),
        [pltpu.VMEM((cuts * ROWS // BLOCK, BLOCK, width), F32)],
    )(plan, own, received, passed, tiles, *layer)


def over_cuts(parts, mine):
    cut = lax.axis_index("cuts")
    total = mine[...]
    for k in range(parts.shape[0]):
        total = total + jnp.where(cut == k, 0.0, parts[k].astype(F32))
    return total


def middle_body(parts, mine, picks, hub_picks, table, out):
    rows = over_cuts(parts, mine).astype(BF16)
    table[...] = rows
    fill_outgoing(rows, picks[...], hub_picks[...], out, DEAD)


def middle(parts, mine, picks, hub_picks):
    width = mine.shape[1]
    return call(
        middle_body,
        (
            jax.ShapeDtypeStruct((ROWS, width), BF16),
            jax.ShapeDtypeStruct((picks.shape[0] // CORES, CORES * SLOT + HUB, width), BF16),
        ),
        [VMEM] * 4,
    )(parts, mine, picks, hub_picks)


def last_body(parts, mine, weight, bias, out):
    total = over_cuts(parts, mine)
    high = total.astype(BF16)
    low = (total - high.astype(F32)).astype(BF16)
    hidden = jnp.dot(high, weight[...], preferred_element_type=F32) + jnp.dot(
        low, weight[...], preferred_element_type=F32
    )
    out[...] = jnp.maximum(hidden + bias[...], 0.0).astype(BF16)


def swap(rows, axis):
    return lax.all_to_all(rows, axis, split_axis=0, concat_axis=0, tiled=True)


def exchange(rows):
    size = lax.axis_size("dom")
    alike = [list(range(core, size, CORES)) for core in range(CORES)]
    received = lax.all_to_all(
        rows, "dom", split_axis=0, concat_axis=0, tiled=True, axis_index_groups=alike
    )
    return received, lax.ppermute(received, "dom", [(i, i ^ 1) for i in range(size)])


def local(
    features,
    weight_one,
    bias_one,
    weight_two,
    bias_two,
    hub_rows,
    halo_rows,
    halo_count,
    tile_target,
    tile_source,
    tile_count,
    tile_values,
):
    cuts = lax.axis_size("cuts")
    halo_rows = halo_rows.reshape(halo_rows.shape[2:]).T
    tiles = tile_values.reshape(tile_values.shape[2:])
    row = lambda x: x.reshape(1, -1)
    outgoing, picks, hub_picks, plan, bias_one, bias_two = pack(
        (row(bias_one), row(bias_two)),
        row(tile_target),
        row(tile_source),
        row(tile_count),
        halo_rows,
        row(halo_count),
        row(hub_rows),
        features,
    )
    plan = plan.reshape(-1)
    parts, mine = tile_sums(features, *exchange(outgoing), plan, tiles, cuts)
    table, outgoing = middle(swap(parts, "cuts"), mine, picks, hub_picks)
    parts, mine = tile_sums(
        table, *exchange(outgoing), plan, tiles, cuts, weight_one, bias_one
    )
    return call(
        last_body,
        jax.ShapeDtypeStruct((ROWS, weight_two.shape[1]), BF16),
        [VMEM] * 4,
    )(swap(parts, "cuts"), mine, weight_two, bias_two)


def solution(mesh):
    return jax.shard_map(
        local,
        mesh=mesh,
        in_specs=(
            P(("dom", "cuts"), None),
            P(),
            P(),
            P(),
            P(),
            P("dom", "cuts", None),
            P("dom", "cuts", None, None),
            P("dom", "cuts", None),
            P("dom", "cuts", None),
            P("dom", "cuts", None),
            P("dom", "cuts"),
            P("dom", "cuts", None, None, None),
        ),
        out_specs=P(("dom", "cuts"), None),
        check_vma=False,
    )
```

time: 124 us -> 115 us (0.927)
  blocking collectives: 62.8 us -> 90.7 us
  waiting for transfers between devices: 29.8 us -> 3.78 us
  starting transfers between devices: 18.5 us -> 11.6 us
  local copies, waits for them, and re-layouts: 4.38 us -> 1.61 us
  Pallas kernels: 6.85 us -> 5.33 us
    all_to_all x0 -> x2, blocking collectives: none -> 65.1 us  [exchange(): lax.all_to_all(rows, 'dom', split_axis=0, concat_axis=0, tiled=True, axis...]
    all_to_all x3 -> x2, blocking collectives: 62.8 us -> 25.6 us  [swap(): return lax.all_to_all(rows, axis, split_axis=0, concat_axis=0, tiled=True)]
    all_to_all x1 -> x0, waiting for transfers between devices: 29.8 us -> none  [swap(): return lax.all_to_all(rows, axis, split_axis=0, concat_axis=0, tiled=True)]
    all_to_all x1 -> x0, starting transfers between devices: 18.5 us -> none  [swap(): return lax.all_to_all(rows, axis, split_axis=0, concat_axis=0, tiled=True)]
    ppermute x0 -> x2, starting transfers between devices: none -> 11.6 us  [exchange(): lax.ppermute(received, 'dom', [(i, i ^ 1) for i in range(size)])]
    ppermute x0 -> x2, waiting for transfers between devices: none -> 3.78 us  [exchange(): lax.ppermute(received, 'dom', [(i, i ^ 1) for i in range(size)])]
    unnamed x23 -> x24, local copies, waits for them, and re-layouts: 4.38 us -> 1.61 us
  transfers between devices with their start and end apart: 1 -> 2, of which waited for: 1 -> 2; matrix products, arithmetic and copies ran while one was open for 0% -> 0% of each run, Pallas kernels for 0% -> 0%
where the time goes in v3:
time: 115 us; the launch traced here: 114 us
  blocking collectives  90.7 us (79%)
  starting transfers between devices  11.6 us (10%)
  Pallas kernels  5.33 us (5%)
  waiting for transfers between devices  3.78 us (3%)
  local copies, waits for them, and re-layouts  1.61 us (1%)
    all_to_all x2, blocking collectives, exchange(): lax.all_to_all(rows, 'dom', split_axis=0, concat_axis=0, tiled=True, axis...  65.1 us
    all_to_all x2, blocking collectives, swap(): return lax.all_to_all(rows, axis, split_axis=0, concat_axis=0, tiled=True)  25.6 us
    ppermute x2, starting transfers between devices, exchange(): lax.ppermute(received, 'dom', [(i, i ^ 1) for i in range(size)])  11.6 us
    ppermute x2, waiting for transfers between devices, exchange(): lax.ppermute(received, 'dom', [(i, i ^ 1) for i in range(size)])  3.78 us
    pallas_call x2, Pallas kernels, tile_sums(): call(sum_body, (jax.ShapeDtypeStruct((cuts, ROWS, width), BF16), jax.Shap...  2.62 us
  transfers between devices with their start and end apart: 2, of which 2 were waited for; matrix products, arithmetic and copies ran while one was open for 0% of the time, Pallas kernels for 0%

profile of v3, /device:TPU:1, one launch (start us, length us, event | category | flops | bytes accessed | tf_op | source)
XLA Modules:
  0.0 113.8 jit_solution(8785530172939881178)
XLA Ops:
  0.7 0.0 copy-start.11
  0.7 0.0 copy-start.7
  0.7 0.6 copy-done.11
  1.3 0.0 copy-done.7
  1.4 0.0 copy-done.10
  1.4 0.0 copy-done.6
  1.4 0.9 copy-done.1
  2.3 1.0 shard_map.118
  3.3 0.0 copy-start
  3.3 0.0 copy-start.2
  3.3 38.2 %all_to_all.20.received = bf16[64,48,128]{2,1,0:T(8,128)(2,1)S(1)} all-to-all(bf16[64,48,128]{2,1,0:T(8,128)(2,1)S(1)} %get-tuple-element.18), channel_id=1, replica_groups={{0,8,16,24,32,40,48,56,64,72,80,88,96,104,112,120,128,136,144,152,160,1..., dimensions={0} | all-to-all | bytes 1572864 | tf_op jit(solution)/shard_map/all_to_all | solution.py:217
  41.6 5.3 %collective-permute-start = (bf16[64,48,128]{2,1,0:T(8,128)(2,1)S(1)}, bf16[64,48,128]{2,1,0:T(8,128)(2,1)S(1)}, u32[]{:S(2)}, u32[]{:S(2)}) collective-permute-start(bf16[64,48,128]{2,1,0:T(8,128)(2,1)S(1)} %all_to_all.20.received), channel_id=1, source_target_pairs={{0,4},{4,0},{8,12},{12,8},{16,20},{20,16},{24,28},{28,24},{32,36},... | collective-permute-start | bytes 2359304 | tf_op jit(solution)/shard_map/ppermute | solution.py:220
  46.9 1.9 %collective-permute-done.passed = bf16[64,48,128]{2,1,0:T(8,128)(2,1)S(1)} collective-permute-done((bf16[64,48,128]{2,1,0:T(8,128)(2,1)S(1)}, bf16[64,48,128]{2,1,0:T(8,128)(2,1)S(1)}, u32[]{:S(2)}, u32[]{:S(2)}) %collective-permute-start) | collective-permute-done | bytes 786464 | tf_op jit(solution)/shard_map/ppermute | solution.py:220
  48.8 1.0 shard_map.119
  49.8 11.0 %all_to_all.21.parts = bf16[4,384,128]{2,1,0:T(8,128)(2,1)S(1)} all-to-all(bf16[4,384,128]{2,1,0:T(8,128)(2,1)S(1)} %get-tuple-element.19), channel_id=1, replica_groups=mesh['dom'=128,'cuts'=4] {'cuts'}, dimensions={0} | all-to-all | bytes 786432 | tf_op jit(solution)/shard_map/all_to_all | solution.py:211
  60.8 0.7 shard_map.120
  61.5 0.0 copy-start.4
  61.5 26.8 %all_to_all.22.received = bf16[64,48,128]{2,1,0:T(8,128)(2,1)S(1)} all-to-all(bf16[64,48,128]{2,1,0:T(8,128)(2,1)S(1)} %get-tuple-element.24), channel_id=1, replica_groups={{0,8,16,24,32,40,48,56,64,72,80,88,96,104,112,120,128,136,144,152,160,1..., dimensions={0} | all-to-all | bytes 1572864 | tf_op jit(solution)/shard_map/all_to_all | solution.py:217
  88.4 6.3 %collective-permute-start.1 = (bf16[64,48,128]{2,1,0:T(8,128)(2,1)S(1)}, bf16[64,48,128]{2,1,0:T(8,128)(2,1)S(1)}, u32[]{:S(2)}, u32[]{:S(2)}) collective-permute-start(bf16[64,48,128]{2,1,0:T(8,128)(2,1)S(1)} %all_to_all.22.received), channel_id=1, source_target_pairs={{0,4},{4,0},{8,12},{12,8},{16,20},{20,16},{24,28},{28,24},{32,36},... | collective-permute-start | bytes 2359304 | tf_op jit(solution)/shard_map/ppermute | solution.py:220
  94.7 1.9 %collective-permute-done.1.passed = bf16[64,48,128]{2,1,0:T(8,128)(2,1)S(1)} collective-permute-done((bf16[64,48,128]{2,1,0:T(8,128)(2,1)S(1)}, bf16[64,48,128]{2,1,0:T(8,128)(2,1)S(1)}, u32[]{:S(2)}, u32[]{:S(2)}) %collective-permute-start.1) | collective-permute-done | bytes 786464 | tf_op jit(solution)/shard_map/ppermute | solution.py:220
  96.6 1.6 %shard_map.121 = (bf16[4,384,256]{2,1,0:T(8,128)(2,1)S(1)}, f32[384,256]{1,0:T(8,128)S(1)}) custom-call(s32[128]{0:T(128)S(1)} %bitcast.15, bf16[384,128]{1,0:T(8,128)(2,1)S(1)} %get-tuple-element.23.own, bf16[64,48,128]{2,1,0:T(8,128)(2,1)S(1)} %all_to_all.22.received, bf16[64,48,128]{2,1,0:T(8,128)(2,1)S(1)} %collective-permute-done.1.passed, ...), custom_call_target="tpu_custom_call" | custom-call | tf_op jit(solution)/shard_map/pallas_call | solution.py:163
  98.2 0.0 copy-start.3
  98.2 14.6 %all_to_all.23.parts = bf16[4,384,256]{2,1,0:T(8,128)(2,1)S(1)} all-to-all(bf16[4,384,256]{2,1,0:T(8,128)(2,1)S(1)} %get-tuple-element.26), channel_id=1, replica_groups=mesh['dom'=128,'cuts'=4] {'cuts'}, dimensions={0} | all-to-all | bytes 1572864 | tf_op jit(solution)/shard_map/all_to_all | solution.py:211
  112.8 1.0 shard_map.122
  (13 shorter events, 0.0 us)
Async XLA Ops:
  0.0 0.7 copy-start.5
  0.7 0.7 copy-start.11
  0.7 0.7 copy-start.7
  0.7 0.7 copy-start.9
  0.7 0.7 copy-start.10
  0.7 0.7 copy-start.6
  0.7 0.7 copy-start.8
  1.4 0.9 copy-start.1
  3.3 45.5 %copy-start = (bf16[1,1,16,128,128]{4,3,2,1,0:T(8,128)(2,1)S(1)}, bf16[1,1,16,128,128]{4,3,2,1,0:T(8,128)(2,1)}, u32[]{:S(2)}) copy-start(bf16[1,1,16,128,128]{4,3,2,1,0:T(8,128)(2,1)} %param.23) | copy-start | bytes 1572868
  3.3 45.5 %copy-start.2 = (bf16[384,128]{1,0:T(8,128)(2,1)S(1)}, bf16[384,128]{1,0:T(8,128)(2,1)}, u32[]{:S(2)}) copy-start(bf16[384,128]{1,0:T(8,128)(2,1)} %own.1) | copy-start | bytes 294916
  41.6 7.2 %collective-permute-start = (bf16[64,48,128]{2,1,0:T(8,128)(2,1)S(1)}, bf16[64,48,128]{2,1,0:T(8,128)(2,1)S(1)}, u32[]{:S(2)}, u32[]{:S(2)}) collective-permute-start(bf16[64,48,128]{2,1,0:T(8,128)(2,1)S(1)} %all_to_all.20.received), channel_id=1, source_target_pairs={{0,4},{4,0},{8,12},{12,8},{16,20},{20,16},{24,28},{28,24},{32,36},... | collective-permute-start | bytes 2359304 | tf_op jit(solution)/shard_map/ppermute | solution.py:220
  61.5 35.0 %copy-start.4 = (bf16[128,256]{1,0:T(8,128)(2,1)S(1)}, bf16[128,256]{1,0:T(8,128)(2,1)}, u32[]{:S(2)}) copy-start(bf16[128,256]{1,0:T(8,128)(2,1)} %rest_0_.1) | copy-start | bytes 196612
  88.4 8.2 %collective-permute-start.1 = (bf16[64,48,128]{2,1,0:T(8,128)(2,1)S(1)}, bf16[64,48,128]{2,1,0:T(8,128)(2,1)S(1)}, u32[]{:S(2)}, u32[]{:S(2)}) collective-permute-start(bf16[64,48,128]{2,1,0:T(8,128)(2,1)S(1)} %all_to_all.22.received), channel_id=1, source_target_pairs={{0,4},{4,0},{8,12},{12,8},{16,20},{20,16},{24,28},{28,24},{32,36},... | collective-permute-start | bytes 2359304 | tf_op jit(solution)/shard_map/ppermute | solution.py:220
  98.2 14.6 %copy-start.3 = (bf16[256,256]{1,0:T(8,128)(2,1)S(1)}, bf16[256,256]{1,0:T(8,128)(2,1)}, u32[]{:S(2)}) copy-start(bf16[256,256]{1,0:T(8,128)(2,1)} %weight.1) | copy-start | bytes 393220

commit v4 on v3

--- a/solution.py
+++ b/solution.py
@@ -70,23 +70,10 @@
 
 
 def pack_body(*refs):
-    count = (len(refs) - 5) // 2
-    sources, (out, picks_out, hubs_out, plan_out) = refs[:count], refs[count : count + 4]
-    kept, sems = refs[count + 4 : -1], refs[-1]
-    copies = [
-        pltpu.make_async_copy(source, place, sems.at[i])
-        for i, (source, place) in enumerate(zip(sources, kept, strict=True))
-    ]
-    for copy in copies:
-        copy.start()
-    for copy in copies:
-        copy.wait()
-    targets, columns, used, halo_rows, halo_count, hub_rows, table = kept[-7:]
-    pieces = [targets[...], columns[...], used[...]]
-    spare = plan_out.shape[1] - sum(piece.shape[1] for piece in pieces)
-    plan_out[...] = jnp.concatenate(
-        [*pieces, jnp.zeros((1, spare), jnp.int32)], axis=1
-    )
+    count = (len(refs) - 4 - 7) // 2
+    handed, operands = refs[:count], refs[count : count + 7]
+    out, picks_out, hubs_out, plan_out, *handed_out = refs[count + 7 :]
+    targets, columns, used, halo_rows, halo_count, hub_rows, table = operands
     slots, parts = halo_rows.shape
     slot = lax.broadcasted_iota(jnp.int32, (slots, parts), 0)
     picks = jnp.where(slot < halo_count[...], halo_rows[...], -1).T
@@ -94,27 +81,28 @@
     picks_out[...] = picks
     hubs_out[...] = hub_picks
     fill_outgoing(table[...], picks, hub_picks, out, 0.0)
+    pieces = [targets[...], columns[...], used[...]]
+    spare = plan_out.shape[1] - sum(piece.shape[1] for piece in pieces)
+    plan_out[...] = jnp.concatenate(
+        [*pieces, jnp.zeros((1, spare), jnp.int32)], axis=1
+    )
+    for source, place in zip(handed, handed_out, strict=True):
+        place[...] = source[...]
 
 
 def pack(handed, *operands):
     slots, parts = operands[-4].shape
-    table = operands[-1]
-    return pl.pallas_call(
+    width = operands[-1].shape[1]
+    return call(
         pack_body,
-        out_shape=(
-            jax.ShapeDtypeStruct((parts // CORES, CORES * SLOT + HUB, table.shape[1]), BF16),
+        (
+            jax.ShapeDtypeStruct((parts // CORES, CORES * SLOT + HUB, width), BF16),
             jax.ShapeDtypeStruct((parts, slots), jnp.int32),
             jax.ShapeDtypeStruct((HUB, ROWS), jnp.int32),
             jax.ShapeDtypeStruct((1, 128), jnp.int32),
             *(jax.ShapeDtypeStruct(x.shape, x.dtype) for x in handed),
         ),
-        in_specs=[spec(pltpu.HBM)] * (len(handed) + len(operands)),
-        out_specs=(spec(VMEM),) * (4 + len(handed)),
-        scratch_shapes=[
-            *(pltpu.VMEM(x.shape, x.dtype) for x in operands),
-            pltpu.SemaphoreType.DMA((len(handed) + len(operands),)),
-        ],
-        compiler_params=pltpu.CompilerParams(vmem_limit_bytes=LIMIT),
+        [VMEM] * (len(handed) + len(operands)),
     )(*handed, *operands)
 
 

time: 115 us -> 115 us (level)
  no operation moved by 1% of the time
where the time goes in v4:
time: 115 us; the launch traced here: 114 us
  blocking collectives  90.7 us (79%)
  starting transfers between devices  11.6 us (10%)
  Pallas kernels  5.11 us (4%)
  waiting for transfers between devices  3.78 us (3%)
  local copies, waits for them, and re-layouts  1.61 us (1%)
    all_to_all x2, blocking collectives, exchange(): lax.all_to_all(rows, 'dom', split_axis=0, concat_axis=0, tiled=True, axis...  65.1 us
    all_to_all x2, blocking collectives, swap(): return lax.all_to_all(rows, axis, split_axis=0, concat_axis=0, tiled=True)  25.6 us
    ppermute x2, starting transfers between devices, exchange(): lax.ppermute(received, 'dom', [(i, i ^ 1) for i in range(size)])  11.6 us
    ppermute x2, waiting for transfers between devices, exchange(): lax.ppermute(received, 'dom', [(i, i ^ 1) for i in range(size)])  3.78 us
    pallas_call x2, Pallas kernels, tile_sums(): call(sum_body, (jax.ShapeDtypeStruct((cuts, ROWS, width), BF16), jax.Shap...  2.63 us
  transfers between devices with their start and end apart: 2, of which 2 were waited for; matrix products, arithmetic and copies ran while one was open for 0% of the time, Pallas kernels for 0%

profile of v4, /device:TPU:1, one launch (start us, length us, event | category | flops | bytes accessed | tf_op | source)
XLA Modules:
  0.0 113.6 jit_solution(582719031153423197)
XLA Ops:
  0.7 0.6 copy-done.11
  1.3 0.0 copy-done.7
  1.4 0.0 copy-done.10
  1.4 0.0 copy-done.6
  1.4 0.9 copy-done.1
  2.3 0.8 shard_map.118
  3.1 0.0 copy-start
  3.1 0.0 copy-start.2
  3.1 38.2 %all_to_all.20.received = bf16[64,48,128]{2,1,0:T(8,128)(2,1)S(1)} all-to-all(bf16[64,48,128]{2,1,0:T(8,128)(2,1)S(1)} %get-tuple-element.18), channel_id=1, replica_groups={{0,8,16,24,32,40,48,56,64,72,80,88,96,104,112,120,128,136,144,152,160,1..., dimensions={0} | all-to-all | bytes 1572864 | tf_op jit(solution)/shard_map/all_to_all | solution.py:205
  41.3 5.3 %collective-permute-start = (bf16[64,48,128]{2,1,0:T(8,128)(2,1)S(1)}, bf16[64,48,128]{2,1,0:T(8,128)(2,1)S(1)}, u32[]{:S(2)}, u32[]{:S(2)}) collective-permute-start(bf16[64,48,128]{2,1,0:T(8,128)(2,1)S(1)} %all_to_all.20.received), channel_id=1, source_target_pairs={{0,4},{4,0},{8,12},{12,8},{16,20},{20,16},{24,28},{28,24},{32,36},... | collective-permute-start | bytes 2359304 | tf_op jit(solution)/shard_map/ppermute | solution.py:208
  46.7 1.9 %collective-permute-done.passed = bf16[64,48,128]{2,1,0:T(8,128)(2,1)S(1)} collective-permute-done((bf16[64,48,128]{2,1,0:T(8,128)(2,1)S(1)}, bf16[64,48,128]{2,1,0:T(8,128)(2,1)S(1)}, u32[]{:S(2)}, u32[]{:S(2)}) %collective-permute-start) | collective-permute-done | bytes 786464 | tf_op jit(solution)/shard_map/ppermute | solution.py:208
  48.6 0.0 copy-done
  48.6 1.0 shard_map.119
  49.6 11.0 %all_to_all.21.parts = bf16[4,384,128]{2,1,0:T(8,128)(2,1)S(1)} all-to-all(bf16[4,384,128]{2,1,0:T(8,128)(2,1)S(1)} %get-tuple-element.19), channel_id=1, replica_groups=mesh['dom'=128,'cuts'=4] {'cuts'}, dimensions={0} | all-to-all | bytes 786432 | tf_op jit(solution)/shard_map/all_to_all | solution.py:199
  60.6 0.7 shard_map.120
  61.3 0.0 copy-start.4
  61.3 26.8 %all_to_all.22.received = bf16[64,48,128]{2,1,0:T(8,128)(2,1)S(1)} all-to-all(bf16[64,48,128]{2,1,0:T(8,128)(2,1)S(1)} %get-tuple-element.24), channel_id=1, replica_groups={{0,8,16,24,32,40,48,56,64,72,80,88,96,104,112,120,128,136,144,152,160,1..., dimensions={0} | all-to-all | bytes 1572864 | tf_op jit(solution)/shard_map/all_to_all | solution.py:205
  88.1 6.3 %collective-permute-start.1 = (bf16[64,48,128]{2,1,0:T(8,128)(2,1)S(1)}, bf16[64,48,128]{2,1,0:T(8,128)(2,1)S(1)}, u32[]{:S(2)}, u32[]{:S(2)}) collective-permute-start(bf16[64,48,128]{2,1,0:T(8,128)(2,1)S(1)} %all_to_all.22.received), channel_id=1, source_target_pairs={{0,4},{4,0},{8,12},{12,8},{16,20},{20,16},{24,28},{28,24},{32,36},... | collective-permute-start | bytes 2359304 | tf_op jit(solution)/shard_map/ppermute | solution.py:208
  94.5 1.9 %collective-permute-done.1.passed = bf16[64,48,128]{2,1,0:T(8,128)(2,1)S(1)} collective-permute-done((bf16[64,48,128]{2,1,0:T(8,128)(2,1)S(1)}, bf16[64,48,128]{2,1,0:T(8,128)(2,1)S(1)}, u32[]{:S(2)}, u32[]{:S(2)}) %collective-permute-start.1) | collective-permute-done | bytes 786464 | tf_op jit(solution)/shard_map/ppermute | solution.py:208
  96.3 1.6 %shard_map.121 = (bf16[4,384,256]{2,1,0:T(8,128)(2,1)S(1)}, f32[384,256]{1,0:T(8,128)S(1)}) custom-call(s32[128]{0:T(128)S(1)} %bitcast.15, bf16[384,128]{1,0:T(8,128)(2,1)S(1)} %get-tuple-element.23.own, bf16[64,48,128]{2,1,0:T(8,128)(2,1)S(1)} %all_to_all.22.received, bf16[64,48,128]{2,1,0:T(8,128)(2,1)S(1)} %collective-permute-done.1.passed, ...), custom_call_target="tpu_custom_call" | custom-call | tf_op jit(solution)/shard_map/pallas_call | solution.py:151
  98.0 0.0 copy-start.3
  98.0 14.6 %all_to_all.23.parts = bf16[4,384,256]{2,1,0:T(8,128)(2,1)S(1)} all-to-all(bf16[4,384,256]{2,1,0:T(8,128)(2,1)S(1)} %get-tuple-element.26), channel_id=1, replica_groups=mesh['dom'=128,'cuts'=4] {'cuts'}, dimensions={0} | all-to-all | bytes 1572864 | tf_op jit(solution)/shard_map/all_to_all | solution.py:199
  112.6 0.0 copy-done.3
  112.6 1.0 shard_map.122
  (13 shorter events, 0.0 us)
Async XLA Ops:
  0.0 0.7 copy-start.5
  0.7 0.7 copy-start.11
  0.7 0.7 copy-start.7
  0.7 0.7 copy-start.9
  0.7 0.7 copy-start.10
  0.7 0.7 copy-start.6
  0.7 0.7 copy-start.8
  1.4 0.9 copy-start.1
  3.1 45.5 %copy-start = (bf16[1,1,16,128,128]{4,3,2,1,0:T(8,128)(2,1)S(1)}, bf16[1,1,16,128,128]{4,3,2,1,0:T(8,128)(2,1)}, u32[]{:S(2)}) copy-start(bf16[1,1,16,128,128]{4,3,2,1,0:T(8,128)(2,1)} %param.23) | copy-start | bytes 1572868
  3.1 45.5 %copy-start.2 = (bf16[384,128]{1,0:T(8,128)(2,1)S(1)}, bf16[384,128]{1,0:T(8,128)(2,1)}, u32[]{:S(2)}) copy-start(bf16[384,128]{1,0:T(8,128)(2,1)} %own.1) | copy-start | bytes 294916
  41.3 7.2 %collective-permute-start = (bf16[64,48,128]{2,1,0:T(8,128)(2,1)S(1)}, bf16[64,48,128]{2,1,0:T(8,128)(2,1)S(1)}, u32[]{:S(2)}, u32[]{:S(2)}) collective-permute-start(bf16[64,48,128]{2,1,0:T(8,128)(2,1)S(1)} %all_to_all.20.received), channel_id=1, source_target_pairs={{0,4},{4,0},{8,12},{12,8},{16,20},{20,16},{24,28},{28,24},{32,36},... | collective-permute-start | bytes 2359304 | tf_op jit(solution)/shard_map/ppermute | solution.py:208
  61.3 35.0 %copy-start.4 = (bf16[128,256]{1,0:T(8,128)(2,1)S(1)}, bf16[128,256]{1,0:T(8,128)(2,1)}, u32[]{:S(2)}) copy-start(bf16[128,256]{1,0:T(8,128)(2,1)} %rest_0_.1) | copy-start | bytes 196612
  88.1 8.2 %collective-permute-start.1 = (bf16[64,48,128]{2,1,0:T(8,128)(2,1)S(1)}, bf16[64,48,128]{2,1,0:T(8,128)(2,1)S(1)}, u32[]{:S(2)}, u32[]{:S(2)}) collective-permute-start(bf16[64,48,128]{2,1,0:T(8,128)(2,1)S(1)} %all_to_all.22.received), channel_id=1, source_target_pairs={{0,4},{4,0},{8,12},{12,8},{16,20},{20,16},{24,28},{28,24},{32,36},... | collective-permute-start | bytes 2359304 | tf_op jit(solution)/shard_map/ppermute | solution.py:208
  98.0 14.6 %copy-start.3 = (bf16[256,256]{1,0:T(8,128)(2,1)S(1)}, bf16[256,256]{1,0:T(8,128)(2,1)}, u32[]{:S(2)}) copy-start(bf16[256,256]{1,0:T(8,128)(2,1)} %weight.1) | copy-start | bytes 393220

commit v5 on v4

--- a/solution.py
+++ b/solution.py
@@ -26,13 +26,14 @@
 LIMIT = 40 * 1024 * 1024
 
 
-def call(body, out_shape, spaces, scratch=()):
+def call(body, out_shape, spaces, scratch=(), cost=None):
     return pl.pallas_call(
         body,
         out_shape=out_shape,
         in_specs=[spec(s) for s in spaces],
         out_specs=jax.tree.map(lambda _: spec(VMEM), out_shape),
         scratch_shapes=list(scratch),
+        cost_estimate=cost,
         compiler_params=pltpu.CompilerParams(vmem_limit_bytes=LIMIT),
     )
 
@@ -69,6 +70,19 @@
         )
 
 
+def spread_body(number, out):
+    out[...] = jnp.full(out.shape, number[0, 0], jnp.int32)
+
+
+def spread(number):
+    return call(
+        spread_body,
+        jax.ShapeDtypeStruct((1, 128), jnp.int32),
+        [SMEM],
+        cost=pl.CostEstimate(flops=10**9, bytes_accessed=4 * 10**6, transcendentals=0),
+    )(number)
+
+
 def pack_body(*refs):
     count = (len(refs) - 4 - 7) // 2
     handed, operands = refs[:count], refs[count : count + 7]
@@ -81,11 +95,10 @@
     picks_out[...] = picks
     hubs_out[...] = hub_picks
     fill_outgoing(table[...], picks, hub_picks, out, 0.0)
-    pieces = [targets[...], columns[...], used[...]]
-    spare = plan_out.shape[1] - sum(piece.shape[1] for piece in pieces)
-    plan_out[...] = jnp.concatenate(
-        [*pieces, jnp.zeros((1, spare), jnp.int32)], axis=1
-    )
+    capacity = targets.shape[1]
+    plan_out[...] = used[...]
+    plan_out[:, :capacity] = targets[...]
+    plan_out[:, capacity : 2 * capacity] = columns[...]
     for source, place in zip(handed, handed_out, strict=True):
         place[...] = source[...]
 
@@ -230,7 +243,7 @@
         (row(bias_one), row(bias_two)),
         row(tile_target),
         row(tile_source),
-        row(tile_count),
+        spread(row(tile_count)),
         halo_rows,
         row(halo_count),
         row(hub_rows),

time: 115 us -> 114 us (level)
  no operation moved by 1% of the time
where the time goes in v5:
time: 114 us; the launch traced here: 113 us
  blocking collectives  90.7 us (80%)
  starting transfers between devices  11.6 us (10%)
  Pallas kernels  5.11 us (4%)
  waiting for transfers between devices  3.78 us (3%)
    all_to_all x2, blocking collectives, exchange(): lax.all_to_all(rows, 'dom', split_axis=0, concat_axis=0, tiled=True, axis...  65.1 us
    all_to_all x2, blocking collectives, swap(): return lax.all_to_all(rows, axis, split_axis=0, concat_axis=0, tiled=True)  25.6 us
    ppermute x2, starting transfers between devices, exchange(): lax.ppermute(received, 'dom', [(i, i ^ 1) for i in range(size)])  11.6 us
    ppermute x2, waiting for transfers between devices, exchange(): lax.ppermute(received, 'dom', [(i, i ^ 1) for i in range(size)])  3.78 us
    pallas_call x2, Pallas kernels, tile_sums(): call(sum_body, (jax.ShapeDtypeStruct((cuts, ROWS, width), BF16), jax.Shap...  2.62 us
  transfers between devices with their start and end apart: 2, of which 2 were waited for; matrix products, arithmetic and copies ran while one was open for 0% of the time, Pallas kernels for 0%

profile of v5, /device:TPU:1, one launch (start us, length us, event | category | flops | bytes accessed | tf_op | source)
XLA Modules:
  0.0 112.9 jit_solution(16966901408063140193)
XLA Ops:
  0.7 0.0 copy-start.1
  0.7 0.0 copy-start.6
  0.7 0.0 copy-start.8
  0.7 0.0 copy-start.4
  0.7 0.0 copy-start.5
  0.7 0.0 copy-start.7
  0.7 0.8 copy-done.1
  1.6 0.0 copy-done.10
  1.6 0.8 shard_map.119
  2.4 0.0 copy-start
  2.4 38.3 %all_to_all.20.received = bf16[64,48,128]{2,1,0:T(8,128)(2,1)S(1)} all-to-all(bf16[64,48,128]{2,1,0:T(8,128)(2,1)S(1)} %get-tuple-element.18), channel_id=1, replica_groups={{0,8,16,24,32,40,48,56,64,72,80,88,96,104,112,120,128,136,144,152,160,1..., dimensions={0} | all-to-all | bytes 1572864 | tf_op jit(solution)/shard_map/all_to_all | solution.py:218
  40.6 5.3 %collective-permute-start = (bf16[64,48,128]{2,1,0:T(8,128)(2,1)S(1)}, bf16[64,48,128]{2,1,0:T(8,128)(2,1)S(1)}, u32[]{:S(2)}, u32[]{:S(2)}) collective-permute-start(bf16[64,48,128]{2,1,0:T(8,128)(2,1)S(1)} %all_to_all.20.received), channel_id=1, source_target_pairs={{0,4},{4,0},{8,12},{12,8},{16,20},{20,16},{24,28},{28,24},{32,36},... | collective-permute-start | bytes 2359304 | tf_op jit(solution)/shard_map/ppermute | solution.py:221
  46.0 1.9 %collective-permute-done.passed = bf16[64,48,128]{2,1,0:T(8,128)(2,1)S(1)} collective-permute-done((bf16[64,48,128]{2,1,0:T(8,128)(2,1)S(1)}, bf16[64,48,128]{2,1,0:T(8,128)(2,1)S(1)}, u32[]{:S(2)}, u32[]{:S(2)}) %collective-permute-start) | collective-permute-done | bytes 786464 | tf_op jit(solution)/shard_map/ppermute | solution.py:221
  47.9 1.0 shard_map.120
  48.8 11.0 %all_to_all.21.parts = bf16[4,384,128]{2,1,0:T(8,128)(2,1)S(1)} all-to-all(bf16[4,384,128]{2,1,0:T(8,128)(2,1)S(1)} %get-tuple-element.19), channel_id=1, replica_groups=mesh['dom'=128,'cuts'=4] {'cuts'}, dimensions={0} | all-to-all | bytes 786432 | tf_op jit(solution)/shard_map/all_to_all | solution.py:212
  59.9 0.7 shard_map.121
  60.6 0.0 copy-start.3
  60.6 26.8 %all_to_all.22.received = bf16[64,48,128]{2,1,0:T(8,128)(2,1)S(1)} all-to-all(bf16[64,48,128]{2,1,0:T(8,128)(2,1)S(1)} %get-tuple-element.24), channel_id=1, replica_groups={{0,8,16,24,32,40,48,56,64,72,80,88,96,104,112,120,128,136,144,152,160,1..., dimensions={0} | all-to-all | bytes 1572864 | tf_op jit(solution)/shard_map/all_to_all | solution.py:218
  87.4 6.3 %collective-permute-start.1 = (bf16[64,48,128]{2,1,0:T(8,128)(2,1)S(1)}, bf16[64,48,128]{2,1,0:T(8,128)(2,1)S(1)}, u32[]{:S(2)}, u32[]{:S(2)}) collective-permute-start(bf16[64,48,128]{2,1,0:T(8,128)(2,1)S(1)} %all_to_all.22.received), channel_id=1, source_target_pairs={{0,4},{4,0},{8,12},{12,8},{16,20},{20,16},{24,28},{28,24},{32,36},... | collective-permute-start | bytes 2359304 | tf_op jit(solution)/shard_map/ppermute | solution.py:221
  93.7 1.9 %collective-permute-done.1.passed = bf16[64,48,128]{2,1,0:T(8,128)(2,1)S(1)} collective-permute-done((bf16[64,48,128]{2,1,0:T(8,128)(2,1)S(1)}, bf16[64,48,128]{2,1,0:T(8,128)(2,1)S(1)}, u32[]{:S(2)}, u32[]{:S(2)}) %collective-permute-start.1) | collective-permute-done | bytes 786464 | tf_op jit(solution)/shard_map/ppermute | solution.py:221
  95.6 1.6 %shard_map.122 = (bf16[4,384,256]{2,1,0:T(8,128)(2,1)S(1)}, f32[384,256]{1,0:T(8,128)S(1)}) custom-call(s32[128]{0:T(128)S(1)} %bitcast.15, bf16[384,128]{1,0:T(8,128)(2,1)S(1)} %get-tuple-element.23.own, bf16[64,48,128]{2,1,0:T(8,128)(2,1)S(1)} %all_to_all.22.received, bf16[64,48,128]{2,1,0:T(8,128)(2,1)S(1)} %collective-permute-done.1.passed, ...), custom_call_target="tpu_custom_call" | custom-call | tf_op jit(solution)/shard_map/pallas_call | solution.py:164
  97.3 0.0 copy-start.2
  97.3 14.6 %all_to_all.23.parts = bf16[4,384,256]{2,1,0:T(8,128)(2,1)S(1)} all-to-all(bf16[4,384,256]{2,1,0:T(8,128)(2,1)S(1)} %get-tuple-element.26), channel_id=1, replica_groups=mesh['dom'=128,'cuts'=4] {'cuts'}, dimensions={0} | all-to-all | bytes 1572864 | tf_op jit(solution)/shard_map/all_to_all | solution.py:212
  111.9 1.0 shard_map.123
  (12 shorter events, 0.0 us)
Async XLA Ops:
  0.7 0.9 copy-start.1
  0.7 0.9 copy-start.6
  0.7 0.9 copy-start.8
  0.7 0.9 copy-start.9
  0.7 0.9 copy-start.10
  0.7 0.8 copy-start.4
  0.7 0.8 copy-start.5
  0.7 0.8 copy-start.7
  2.4 45.5 %copy-start = (bf16[1,1,16,128,128]{4,3,2,1,0:T(8,128)(2,1)S(1)}, bf16[1,1,16,128,128]{4,3,2,1,0:T(8,128)(2,1)}, u32[]{:S(2)}) copy-start(bf16[1,1,16,128,128]{4,3,2,1,0:T(8,128)(2,1)} %param.23) | copy-start | bytes 1572868
  40.6 7.2 %collective-permute-start = (bf16[64,48,128]{2,1,0:T(8,128)(2,1)S(1)}, bf16[64,48,128]{2,1,0:T(8,128)(2,1)S(1)}, u32[]{:S(2)}, u32[]{:S(2)}) collective-permute-start(bf16[64,48,128]{2,1,0:T(8,128)(2,1)S(1)} %all_to_all.20.received), channel_id=1, source_target_pairs={{0,4},{4,0},{8,12},{12,8},{16,20},{20,16},{24,28},{28,24},{32,36},... | collective-permute-start | bytes 2359304 | tf_op jit(solution)/shard_map/ppermute | solution.py:221
  60.6 35.0 %copy-start.3 = (bf16[128,256]{1,0:T(8,128)(2,1)S(1)}, bf16[128,256]{1,0:T(8,128)(2,1)}, u32[]{:S(2)}) copy-start(bf16[128,256]{1,0:T(8,128)(2,1)} %rest_0_.1) | copy-start | bytes 196612
  87.4 8.2 %collective-permute-start.1 = (bf16[64,48,128]{2,1,0:T(8,128)(2,1)S(1)}, bf16[64,48,128]{2,1,0:T(8,128)(2,1)S(1)}, u32[]{:S(2)}, u32[]{:S(2)}) collective-permute-start(bf16[64,48,128]{2,1,0:T(8,128)(2,1)S(1)} %all_to_all.22.received), channel_id=1, source_target_pairs={{0,4},{4,0},{8,12},{12,8},{16,20},{20,16},{24,28},{28,24},{32,36},... | collective-permute-start | bytes 2359304 | tf_op jit(solution)/shard_map/ppermute | solution.py:221
  97.3 14.6 %copy-start.2 = (bf16[256,256]{1,0:T(8,128)(2,1)S(1)}, bf16[256,256]{1,0:T(8,128)(2,1)}, u32[]{:S(2)}) copy-start(bf16[256,256]{1,0:T(8,128)(2,1)} %weight.1) | copy-start | bytes 393220

commit v6 on v4

--- a/solution.py
+++ b/solution.py
@@ -26,13 +26,14 @@
 LIMIT = 40 * 1024 * 1024
 
 
-def call(body, out_shape, spaces, scratch=()):
+def call(body, out_shape, spaces, scratch=(), cost=None):
     return pl.pallas_call(
         body,
         out_shape=out_shape,
         in_specs=[spec(s) for s in spaces],
         out_specs=jax.tree.map(lambda _: spec(VMEM), out_shape),
         scratch_shapes=list(scratch),
+        cost_estimate=cost,
         compiler_params=pltpu.CompilerParams(vmem_limit_bytes=LIMIT),
     )
 
@@ -69,41 +70,60 @@
         )
 
 
+def slots_body(out):
+    out[...] = lax.broadcasted_iota(jnp.int32, out.shape, 0)
+
+
+def slot_numbers(slots, parts):
+    return call(
+        slots_body,
+        jax.ShapeDtypeStruct((slots, parts), jnp.int32),
+        [],
+        cost=pl.CostEstimate(flops=10**9, bytes_accessed=4 * 10**6, transcendentals=0),
+    )()
+
+
 def pack_body(*refs):
-    count = (len(refs) - 4 - 7) // 2
-    handed, operands = refs[:count], refs[count : count + 7]
-    out, picks_out, hubs_out, plan_out, *handed_out = refs[count + 7 :]
-    targets, columns, used, halo_rows, halo_count, hub_rows, table = operands
-    slots, parts = halo_rows.shape
-    slot = lax.broadcasted_iota(jnp.int32, (slots, parts), 0)
-    picks = jnp.where(slot < halo_count[...], halo_rows[...], -1).T
+    count = (len(refs) - 3 - 5) // 2
+    handed, (slot, halo_rows, halo_count, hub_rows, table) = refs[:count], refs[count : count + 5]
+    out, picks_out, hubs_out, *handed_out = refs[count + 5 :]
+    picks = jnp.where(slot[...] < halo_count[...], halo_rows[...], -1).T
     hub_picks = jnp.broadcast_to(column(hub_rows[...], HUB), (HUB, ROWS))
     picks_out[...] = picks
     hubs_out[...] = hub_picks
     fill_outgoing(table[...], picks, hub_picks, out, 0.0)
-    pieces = [targets[...], columns[...], used[...]]
-    spare = plan_out.shape[1] - sum(piece.shape[1] for piece in pieces)
-    plan_out[...] = jnp.concatenate(
-        [*pieces, jnp.zeros((1, spare), jnp.int32)], axis=1
-    )
     for source, place in zip(handed, handed_out, strict=True):
         place[...] = source[...]
 
 
-def pack(handed, *operands):
-    slots, parts = operands[-4].shape
-    width = operands[-1].shape[1]
+def pack(handed, halo_rows, halo_count, hub_rows, table):
+    slots, parts = halo_rows.shape
+    operands = (slot_numbers(slots, parts), halo_rows, halo_count, hub_rows, table)
     return call(
         pack_body,
         (
-            jax.ShapeDtypeStruct((parts // CORES, CORES * SLOT + HUB, width), BF16),
+            jax.ShapeDtypeStruct(
+                (parts // CORES, CORES * SLOT + HUB, table.shape[1]), BF16
+            ),
             jax.ShapeDtypeStruct((parts, slots), jnp.int32),
             jax.ShapeDtypeStruct((HUB, ROWS), jnp.int32),
-            jax.ShapeDtypeStruct((1, 128), jnp.int32),
             *(jax.ShapeDtypeStruct(x.shape, x.dtype) for x in handed),
         ),
         [VMEM] * (len(handed) + len(operands)),
     )(*handed, *operands)
+
+
+def plan_body(targets, columns, used, out):
+    capacity = targets.shape[1]
+    out[...] = jnp.broadcast_to(used[...], out.shape)
+    out[:, :capacity] = targets[...]
+    out[:, capacity : 2 * capacity] = columns[...]
+
+
+def tile_plan(targets, columns, used):
+    return call(
+        plan_body, jax.ShapeDtypeStruct((1, 128), jnp.int32), [VMEM] * 3
+    )(targets, columns, used)
 
 
 def sum_body(plan, own, received, passed, tiles, *rest):
@@ -226,17 +246,14 @@
     halo_rows = halo_rows.reshape(halo_rows.shape[2:]).T
     tiles = tile_values.reshape(tile_values.shape[2:])
     row = lambda x: x.reshape(1, -1)
-    outgoing, picks, hub_picks, plan, bias_one, bias_two = pack(
+    outgoing, picks, hub_picks, bias_one, bias_two = pack(
         (row(bias_one), row(bias_two)),
-        row(tile_target),
-        row(tile_source),
-        row(tile_count),
         halo_rows,
         row(halo_count),
         row(hub_rows),
         features,
     )
-    plan = plan.reshape(-1)
+    plan = tile_plan(row(tile_target), row(tile_source), row(tile_count)).reshape(-1)
     parts, mine = tile_sums(features, *exchange(outgoing), plan, tiles, cuts)
     table, outgoing = middle(swap(parts, "cuts"), mine, picks, hub_picks)
     parts, mine = tile_sums(

time: 115 us -> 113 us (0.983)
  waiting for transfers between devices: 3.78 us -> 2.38 us
    ppermute x2, waiting for transfers between devices: 3.78 us -> 2.38 us  [exchange(): lax.ppermute(received, 'dom', [(i, i ^ 1) for i in range(size)])]
where the time goes in v6:
time: 113 us; the launch traced here: 112 us
  blocking collectives  90.7 us (80%)
  starting transfers between devices  11.6 us (10%)
  Pallas kernels  5.2 us (5%)
  waiting for transfers between devices  2.38 us (2%)
  local copies, waits for them, and re-layouts  1.54 us (1%)
    all_to_all x2, blocking collectives, exchange(): lax.all_to_all(rows, 'dom', split_axis=0, concat_axis=0, tiled=True, axis...  65.1 us
    all_to_all x2, blocking collectives, swap(): return lax.all_to_all(rows, axis, split_axis=0, concat_axis=0, tiled=True)  25.6 us
    ppermute x2, starting transfers between devices, exchange(): lax.ppermute(received, 'dom', [(i, i ^ 1) for i in range(size)])  11.6 us
    pallas_call x2, Pallas kernels, tile_sums(): call(sum_body, (jax.ShapeDtypeStruct((cuts, ROWS, width), BF16), jax.Shap...  2.63 us
    ppermute x2, waiting for transfers between devices, exchange(): lax.ppermute(received, 'dom', [(i, i ^ 1) for i in range(size)])  2.38 us
  transfers between devices with their start and end apart: 2, of which 2 were waited for; matrix products, arithmetic and copies ran while one was open for 0% of the time, Pallas kernels for 0%

profile of v6, /device:TPU:1, one launch (start us, length us, event | category | flops | bytes accessed | tf_op | source)
XLA Modules:
  0.0 112.2 jit_solution(2908063205766634127)
XLA Ops:
  0.0 0.0 copy-start.4
  0.0 0.0 copy-start.5
  0.1 0.8 copy-done.1
  0.9 0.8 shard_map.120
  1.7 0.0 copy-start
  1.7 38.2 %all_to_all.20.received = bf16[64,48,128]{2,1,0:T(8,128)(2,1)S(1)} all-to-all(bf16[64,48,128]{2,1,0:T(8,128)(2,1)S(1)} %get-tuple-element.16), channel_id=1, replica_groups={{0,8,16,24,32,40,48,56,64,72,80,88,96,104,112,120,128,136,144,152,160,1..., dimensions={0} | all-to-all | bytes 1572864 | tf_op jit(solution)/shard_map/all_to_all | solution.py:225
  40.0 5.3 %collective-permute-start = (bf16[64,48,128]{2,1,0:T(8,128)(2,1)S(1)}, bf16[64,48,128]{2,1,0:T(8,128)(2,1)S(1)}, u32[]{:S(2)}, u32[]{:S(2)}) collective-permute-start(bf16[64,48,128]{2,1,0:T(8,128)(2,1)S(1)} %all_to_all.20.received), channel_id=1, source_target_pairs={{0,4},{4,0},{8,12},{12,8},{16,20},{20,16},{24,28},{28,24},{32,36},... | collective-permute-start | bytes 2359304 | tf_op jit(solution)/shard_map/ppermute | solution.py:228
  45.9 0.0 copy-start.9
  45.9 0.0 copy-start.10
  46.0 0.6 copy-done.9
  46.6 0.0 copy-done.10
  46.6 0.1 shard_map.118
  46.7 0.5 collective-permute-done.passed
  47.2 1.0 shard_map.121
  48.2 11.0 %all_to_all.21.parts = bf16[4,384,128]{2,1,0:T(8,128)(2,1)S(1)} all-to-all(bf16[4,384,128]{2,1,0:T(8,128)(2,1)S(1)} %get-tuple-element.17), channel_id=1, replica_groups=mesh['dom'=128,'cuts'=4] {'cuts'}, dimensions={0} | all-to-all | bytes 786432 | tf_op jit(solution)/shard_map/all_to_all | solution.py:219
  59.2 0.7 shard_map.122
  59.9 0.0 copy-start.3
  59.9 26.8 %all_to_all.22.received = bf16[64,48,128]{2,1,0:T(8,128)(2,1)S(1)} all-to-all(bf16[64,48,128]{2,1,0:T(8,128)(2,1)S(1)} %get-tuple-element.22), channel_id=1, replica_groups={{0,8,16,24,32,40,48,56,64,72,80,88,96,104,112,120,128,136,144,152,160,1..., dimensions={0} | all-to-all | bytes 1572864 | tf_op jit(solution)/shard_map/all_to_all | solution.py:225
  86.7 6.3 %collective-permute-start.1 = (bf16[64,48,128]{2,1,0:T(8,128)(2,1)S(1)}, bf16[64,48,128]{2,1,0:T(8,128)(2,1)S(1)}, u32[]{:S(2)}, u32[]{:S(2)}) collective-permute-start(bf16[64,48,128]{2,1,0:T(8,128)(2,1)S(1)} %all_to_all.22.received), channel_id=1, source_target_pairs={{0,4},{4,0},{8,12},{12,8},{16,20},{20,16},{24,28},{28,24},{32,36},... | collective-permute-start | bytes 2359304 | tf_op jit(solution)/shard_map/ppermute | solution.py:228
  93.0 1.9 %collective-permute-done.1.passed = bf16[64,48,128]{2,1,0:T(8,128)(2,1)S(1)} collective-permute-done((bf16[64,48,128]{2,1,0:T(8,128)(2,1)S(1)}, bf16[64,48,128]{2,1,0:T(8,128)(2,1)S(1)}, u32[]{:S(2)}, u32[]{:S(2)}) %collective-permute-start.1) | collective-permute-done | bytes 786464 | tf_op jit(solution)/shard_map/ppermute | solution.py:228
  94.9 1.6 %shard_map.123 = (bf16[4,384,256]{2,1,0:T(8,128)(2,1)S(1)}, f32[384,256]{1,0:T(8,128)S(1)}) custom-call(s32[128]{0:T(128)S(1)} %bitcast.15, bf16[384,128]{1,0:T(8,128)(2,1)S(1)} %get-tuple-element.21.own, bf16[64,48,128]{2,1,0:T(8,128)(2,1)S(1)} %all_to_all.22.received, bf16[64,48,128]{2,1,0:T(8,128)(2,1)S(1)} %collective-permute-done.1.passed, ...), custom_call_target="tpu_custom_call" | custom-call | tf_op jit(solution)/shard_map/pallas_call | solution.py:171
  96.6 0.0 copy-start.2
  96.6 14.6 %all_to_all.23.parts = bf16[4,384,256]{2,1,0:T(8,128)(2,1)S(1)} all-to-all(bf16[4,384,256]{2,1,0:T(8,128)(2,1)S(1)} %get-tuple-element.24), channel_id=1, replica_groups=mesh['dom'=128,'cuts'=4] {'cuts'}, dimensions={0} | all-to-all | bytes 1572864 | tf_op jit(solution)/shard_map/all_to_all | solution.py:219
  111.2 1.0 shard_map.124
  (13 shorter events, 0.0 us)
Async XLA Ops:
  0.0 0.9 copy-start.1
  0.0 0.9 copy-start.6
  0.0 0.9 copy-start.7
  0.0 0.9 copy-start.8
  0.0 0.9 copy-start.4
  0.0 0.9 copy-start.5
  1.7 45.5 %copy-start = (bf16[1,1,16,128,128]{4,3,2,1,0:T(8,128)(2,1)S(1)}, bf16[1,1,16,128,128]{4,3,2,1,0:T(8,128)(2,1)}, u32[]{:S(2)}) copy-start(bf16[1,1,16,128,128]{4,3,2,1,0:T(8,128)(2,1)} %param.23) | copy-start | bytes 1572868
  40.0 7.2 %collective-permute-start = (bf16[64,48,128]{2,1,0:T(8,128)(2,1)S(1)}, bf16[64,48,128]{2,1,0:T(8,128)(2,1)S(1)}, u32[]{:S(2)}, u32[]{:S(2)}) collective-permute-start(bf16[64,48,128]{2,1,0:T(8,128)(2,1)S(1)} %all_to_all.20.received), channel_id=1, source_target_pairs={{0,4},{4,0},{8,12},{12,8},{16,20},{20,16},{24,28},{28,24},{32,36},... | collective-permute-start | bytes 2359304 | tf_op jit(solution)/shard_map/ppermute | solution.py:228
  45.9 0.7 copy-start.9
  45.9 0.7 copy-start.10
  59.9 35.0 %copy-start.3 = (bf16[128,256]{1,0:T(8,128)(2,1)S(1)}, bf16[128,256]{1,0:T(8,128)(2,1)}, u32[]{:S(2)}) copy-start(bf16[128,256]{1,0:T(8,128)(2,1)} %rest_0_.1) | copy-start | bytes 196612
  86.7 8.2 %collective-permute-start.1 = (bf16[64,48,128]{2,1,0:T(8,128)(2,1)S(1)}, bf16[64,48,128]{2,1,0:T(8,128)(2,1)S(1)}, u32[]{:S(2)}, u32[]{:S(2)}) collective-permute-start(bf16[64,48,128]{2,1,0:T(8,128)(2,1)S(1)} %all_to_all.22.received), channel_id=1, source_target_pairs={{0,4},{4,0},{8,12},{12,8},{16,20},{20,16},{24,28},{28,24},{32,36},... | collective-permute-start | bytes 2359304 | tf_op jit(solution)/shard_map/ppermute | solution.py:228
  96.6 14.6 %copy-start.2 = (bf16[256,256]{1,0:T(8,128)(2,1)S(1)}, bf16[256,256]{1,0:T(8,128)(2,1)}, u32[]{:S(2)}) copy-start(bf16[256,256]{1,0:T(8,128)(2,1)} %weight.1) | copy-start | bytes 393220

commit v7 on v6

--- a/solution.py
+++ b/solution.py
@@ -1,3 +1,5 @@
+import functools
+
 import jax
 import jax.numpy as jnp
 from jax import lax
@@ -11,6 +13,7 @@
 BLOCK = 128
 CHUNK = 16
 CORES = 2
+HIDDEN_ROWS = 512
 DEAD = 2.0**100
 DEAD_LIMIT = 2.0**50
 VMEM = pltpu.VMEM
@@ -126,8 +129,8 @@
     )(targets, columns, used)
 
 
-def sum_body(plan, own, received, passed, tiles, *rest):
-    *layer, out, mine, total = rest
+def sum_body(layers, plan, own, received, passed, tiles, *rest):
+    layer, (out, mine, total, *scratch) = rest[:layers], rest[layers:]
     total[...] = jnp.zeros_like(total)
     capacity = tiles.shape[0]
     group = BLOCK // (CORES * SLOT)
@@ -135,7 +138,8 @@
     core = lax.rem(lax.axis_index("dom"), CORES)
     own_blocks = ROWS // BLOCK
     used = plan[2 * capacity]
-    for i in range(capacity):
+
+    def source_rows(i):
         col = plan[capacity + i]
         here = jnp.minimum(col, own_blocks - 1)
         local_rows = own[pl.ds(pl.multiple_of(here * BLOCK, BLOCK), BLOCK), :]
@@ -149,14 +153,22 @@
             [jnp.where(core == 0, same, other), jnp.where(core == 0, other, same)],
             axis=1,
         ).reshape(BLOCK, own.shape[1])
-        rows = jnp.where(col < own_blocks, local_rows, remote_rows)
-        if layer:
-            weight, bias = layer
+        return jnp.where(col < own_blocks, local_rows, remote_rows)
+
+    if layer:
+        (weight, bias), (picked, values) = layer, scratch
+        for i in range(capacity):
+            picked[i * BLOCK : (i + 1) * BLOCK] = source_rows(i)
+        for first in range(0, capacity * BLOCK, HIDDEN_ROWS):
+            span = pl.ds(first, HIDDEN_ROWS)
+            rows = picked[span]
             hidden = jnp.dot(rows, weight[...], preferred_element_type=F32)
             hidden = jnp.maximum(hidden + bias[...], 0.0)
             live = rows.astype(F32) < DEAD_LIMIT
             live = jnp.concatenate([live] * (hidden.shape[1] // live.shape[1]), axis=1)
-            rows = jnp.where(live, hidden, 0.0).astype(BF16)
+            values[span] = jnp.where(live, hidden, 0.0).astype(BF16)
+    for i in range(capacity):
+        rows = values[i * BLOCK : (i + 1) * BLOCK] if layer else source_rows(i)
         term = jnp.dot(tiles[i], rows, preferred_element_type=F32)
         row = plan[i]
         total[row] = total[row] + jnp.where(i < used, term, 0.0)
@@ -168,14 +180,18 @@
 
 def tile_sums(own, received, passed, plan, tiles, cuts, *layer):
     width = layer[0].shape[1] if layer else own.shape[1]
-    return call(
-        sum_body,
+    rows = tiles.shape[0] * BLOCK
+    scratch = [pltpu.VMEM((cuts * ROWS // BLOCK, BLOCK, width), F32)]
+    if layer:
+        scratch += [pltpu.VMEM((rows, own.shape[1]), BF16), pltpu.VMEM((rows, width), BF16)]
+    return call(
+        functools.partial(sum_body, len(layer)),
         (
             jax.ShapeDtypeStruct((cuts, ROWS, width), BF16),
             jax.ShapeDtypeStruct((ROWS, width), F32),
         ),
         [SMEM] + [VMEM] * (4 + len(layer)),
-        [pltpu.VMEM((cuts * ROWS // BLOCK, BLOCK, width), F32)],
+        scratch,
     )(plan, own, received, passed, tiles, *layer)
 
 

time: 113 us -> 113 us (level)
  no operation moved by 1% of the time
where the time goes in v7:
time: 113 us; the launch traced here: 112 us
  blocking collectives  90.7 us (80%)
  starting transfers between devices  11.6 us (10%)
  Pallas kernels  5.06 us (4%)
  waiting for transfers between devices  2.38 us (2%)
  local copies, waits for them, and re-layouts  1.54 us (1%)
    all_to_all x2, blocking collectives, exchange(): lax.all_to_all(rows, 'dom', split_axis=0, concat_axis=0, tiled=True, axis...  65.1 us
    all_to_all x2, blocking collectives, swap(): return lax.all_to_all(rows, axis, split_axis=0, concat_axis=0, tiled=True)  25.6 us
    ppermute x2, starting transfers between devices, exchange(): lax.ppermute(received, 'dom', [(i, i ^ 1) for i in range(size)])  11.6 us
    pallas_call x2, Pallas kernels, tile_sums(): call(functools.partial(sum_body, len(layer)), (jax.ShapeDtypeStruct((cuts...  2.49 us
    ppermute x2, waiting for transfers between devices, exchange(): lax.ppermute(received, 'dom', [(i, i ^ 1) for i in range(size)])  2.38 us
  transfers between devices with their start and end apart: 2, of which 2 were waited for; matrix products, arithmetic and copies ran while one was open for 0% of the time, Pallas kernels for 0%

profile of v7, /device:TPU:1, one launch (start us, length us, event | category | flops | bytes accessed | tf_op | source)
XLA Modules:
  0.0 112.1 jit_solution(7382421954285795121)
XLA Ops:
  0.0 0.0 copy-start.4
  0.0 0.0 copy-start.5
  0.1 0.8 copy-done.1
  0.9 0.8 shard_map.120
  1.7 0.0 copy-start
  1.7 38.2 %all_to_all.20.received = bf16[64,48,128]{2,1,0:T(8,128)(2,1)S(1)} all-to-all(bf16[64,48,128]{2,1,0:T(8,128)(2,1)S(1)} %get-tuple-element.16), channel_id=1, replica_groups={{0,8,16,24,32,40,48,56,64,72,80,88,96,104,112,120,128,136,144,152,160,1..., dimensions={0} | all-to-all | bytes 1572864 | tf_op jit(solution)/shard_map/all_to_all | solution.py:241
  40.0 5.3 %collective-permute-start = (bf16[64,48,128]{2,1,0:T(8,128)(2,1)S(1)}, bf16[64,48,128]{2,1,0:T(8,128)(2,1)S(1)}, u32[]{:S(2)}, u32[]{:S(2)}) collective-permute-start(bf16[64,48,128]{2,1,0:T(8,128)(2,1)S(1)} %all_to_all.20.received), channel_id=1, source_target_pairs={{0,4},{4,0},{8,12},{12,8},{16,20},{20,16},{24,28},{28,24},{32,36},... | collective-permute-start | bytes 2359304 | tf_op jit(solution)/shard_map/ppermute | solution.py:244
  45.9 0.0 copy-start.9
  45.9 0.0 copy-start.10
  46.0 0.6 copy-done.9
  46.6 0.0 copy-done.10
  46.6 0.1 shard_map.118
  46.7 0.5 collective-permute-done.passed
  47.2 1.0 shard_map.121
  48.2 11.0 %all_to_all.21.parts = bf16[4,384,128]{2,1,0:T(8,128)(2,1)S(1)} all-to-all(bf16[4,384,128]{2,1,0:T(8,128)(2,1)S(1)} %get-tuple-element.17), channel_id=1, replica_groups=mesh['dom'=128,'cuts'=4] {'cuts'}, dimensions={0} | all-to-all | bytes 786432 | tf_op jit(solution)/shard_map/all_to_all | solution.py:235
  59.2 0.7 shard_map.122
  59.9 0.0 copy-start.3
  59.9 26.9 %all_to_all.22.received = bf16[64,48,128]{2,1,0:T(8,128)(2,1)S(1)} all-to-all(bf16[64,48,128]{2,1,0:T(8,128)(2,1)S(1)} %get-tuple-element.22), channel_id=1, replica_groups={{0,8,16,24,32,40,48,56,64,72,80,88,96,104,112,120,128,136,144,152,160,1..., dimensions={0} | all-to-all | bytes 1572864 | tf_op jit(solution)/shard_map/all_to_all | solution.py:241
  86.8 6.3 %collective-permute-start.1 = (bf16[64,48,128]{2,1,0:T(8,128)(2,1)S(1)}, bf16[64,48,128]{2,1,0:T(8,128)(2,1)S(1)}, u32[]{:S(2)}, u32[]{:S(2)}) collective-permute-start(bf16[64,48,128]{2,1,0:T(8,128)(2,1)S(1)} %all_to_all.22.received), channel_id=1, source_target_pairs={{0,4},{4,0},{8,12},{12,8},{16,20},{20,16},{24,28},{28,24},{32,36},... | collective-permute-start | bytes 2359304 | tf_op jit(solution)/shard_map/ppermute | solution.py:244
  93.1 1.9 %collective-permute-done.1.passed = bf16[64,48,128]{2,1,0:T(8,128)(2,1)S(1)} collective-permute-done((bf16[64,48,128]{2,1,0:T(8,128)(2,1)S(1)}, bf16[64,48,128]{2,1,0:T(8,128)(2,1)S(1)}, u32[]{:S(2)}, u32[]{:S(2)}) %collective-permute-start.1) | collective-permute-done | bytes 786464 | tf_op jit(solution)/shard_map/ppermute | solution.py:244
  95.0 1.5 %shard_map.123 = (bf16[4,384,256]{2,1,0:T(8,128)(2,1)S(1)}, f32[384,256]{1,0:T(8,128)S(1)}) custom-call(s32[128]{0:T(128)S(1)} %bitcast.15, bf16[384,128]{1,0:T(8,128)(2,1)S(1)} %get-tuple-element.21.own, bf16[64,48,128]{2,1,0:T(8,128)(2,1)S(1)} %all_to_all.22.received, bf16[64,48,128]{2,1,0:T(8,128)(2,1)S(1)} %collective-permute-done.1.passed, ...), custom_call_target="tpu_custom_call" | custom-call | tf_op jit(solution)/shard_map/pallas_call | solution.py:187
  96.5 0.0 copy-start.2
  96.5 14.6 %all_to_all.23.parts = bf16[4,384,256]{2,1,0:T(8,128)(2,1)S(1)} all-to-all(bf16[4,384,256]{2,1,0:T(8,128)(2,1)S(1)} %get-tuple-element.24), channel_id=1, replica_groups=mesh['dom'=128,'cuts'=4] {'cuts'}, dimensions={0} | all-to-all | bytes 1572864 | tf_op jit(solution)/shard_map/all_to_all | solution.py:235
  111.1 1.0 shard_map.124
  (13 shorter events, 0.0 us)
Async XLA Ops:
  0.0 0.9 copy-start.1
  0.0 0.9 copy-start.6
  0.0 0.9 copy-start.7
  0.0 0.9 copy-start.8
  0.0 0.9 copy-start.4
  0.0 0.9 copy-start.5
  1.7 45.5 %copy-start = (bf16[1,1,16,128,128]{4,3,2,1,0:T(8,128)(2,1)S(1)}, bf16[1,1,16,128,128]{4,3,2,1,0:T(8,128)(2,1)}, u32[]{:S(2)}) copy-start(bf16[1,1,16,128,128]{4,3,2,1,0:T(8,128)(2,1)} %param.23) | copy-start | bytes 1572868
  40.0 7.2 %collective-permute-start = (bf16[64,48,128]{2,1,0:T(8,128)(2,1)S(1)}, bf16[64,48,128]{2,1,0:T(8,128)(2,1)S(1)}, u32[]{:S(2)}, u32[]{:S(2)}) collective-permute-start(bf16[64,48,128]{2,1,0:T(8,128)(2,1)S(1)} %all_to_all.20.received), channel_id=1, source_target_pairs={{0,4},{4,0},{8,12},{12,8},{16,20},{20,16},{24,28},{28,24},{32,36},... | collective-permute-start | bytes 2359304 | tf_op jit(solution)/shard_map/ppermute | solution.py:244
  45.9 0.7 copy-start.9
  45.9 0.7 copy-start.10
  59.9 35.1 %copy-start.3 = (bf16[128,256]{1,0:T(8,128)(2,1)S(1)}, bf16[128,256]{1,0:T(8,128)(2,1)}, u32[]{:S(2)}) copy-start(bf16[128,256]{1,0:T(8,128)(2,1)} %rest_0_.1) | copy-start | bytes 196612
  86.8 8.2 %collective-permute-start.1 = (bf16[64,48,128]{2,1,0:T(8,128)(2,1)S(1)}, bf16[64,48,128]{2,1,0:T(8,128)(2,1)S(1)}, u32[]{:S(2)}, u32[]{:S(2)}) collective-permute-start(bf16[64,48,128]{2,1,0:T(8,128)(2,1)S(1)} %all_to_all.22.received), channel_id=1, source_target_pairs={{0,4},{4,0},{8,12},{12,8},{16,20},{20,16},{24,28},{28,24},{32,36},... | collective-permute-start | bytes 2359304 | tf_op jit(solution)/shard_map/ppermute | solution.py:244
  96.5 14.6 %copy-start.2 = (bf16[256,256]{1,0:T(8,128)(2,1)S(1)}, bf16[256,256]{1,0:T(8,128)(2,1)}, u32[]{:S(2)}) copy-start(bf16[256,256]{1,0:T(8,128)(2,1)} %weight.1) | copy-start | bytes 393220

commit v8 on v6

--- a/solution.py
+++ b/solution.py
@@ -132,7 +132,7 @@
     capacity = tiles.shape[0]
     group = BLOCK // (CORES * SLOT)
     groups = received.shape[0] // group
-    core = lax.rem(lax.axis_index("dom"), CORES)
+    core = lax.axis_index("core")
     own_blocks = ROWS // BLOCK
     used = plan[2 * capacity]
     for i in range(capacity):
@@ -220,12 +220,8 @@
 
 
 def exchange(rows):
-    size = lax.axis_size("dom")
-    alike = [list(range(core, size, CORES)) for core in range(CORES)]
-    received = lax.all_to_all(
-        rows, "dom", split_axis=0, concat_axis=0, tiled=True, axis_index_groups=alike
-    )
-    return received, lax.ppermute(received, "dom", [(i, i ^ 1) for i in range(size)])
+    received = swap(rows, "chip")
+    return received, lax.ppermute(received, "core", [(0, 1), (1, 0)])
 
 
 def local(
@@ -267,23 +263,28 @@
 
 
 def solution(mesh):
+    cuts = mesh.shape["cuts"]
+    chips = jax.sharding.Mesh(
+        mesh.devices.reshape(-1, CORES, cuts), ("chip", "core", "cuts")
+    )
+    dom = ("chip", "core")
     return jax.shard_map(
         local,
-        mesh=mesh,
+        mesh=chips,
         in_specs=(
-            P(("dom", "cuts"), None),
-            P(),
-            P(),
-            P(),
-            P(),
-            P("dom", "cuts", None),
-            P("dom", "cuts", None, None),
-            P("dom", "cuts", None),
-            P("dom", "cuts", None),
-            P("dom", "cuts", None),
-            P("dom", "cuts"),
-            P("dom", "cuts", None, None, None),
-        ),
-        out_specs=P(("dom", "cuts"), None),
+            P((*dom, "cuts"), None),
+            P(),
+            P(),
+            P(),
+            P(),
+            P(dom, "cuts", None),
+            P(dom, "cuts", None, None),
+            P(dom, "cuts", None),
+            P(dom, "cuts", None),
+            P(dom, "cuts", None),
+            P(dom, "cuts"),
+            P(dom, "cuts", None, None, None),
+        ),
+        out_specs=P((*dom, "cuts"), None),
         check_vma=False,
     )

time: 113 us -> 113 us (level)
    all_to_all x2 -> x4, blocking collectives: 25.6 us -> 90.7 us  [swap(): return lax.all_to_all(rows, axis, split_axis=0, concat_axis=0, tiled=True)]
    all_to_all x2 -> x0, blocking collectives: 65.1 us -> none  [exchange(): lax.all_to_all(rows, 'dom', split_axis=0, concat_axis=0, tiled=True, axis...]
where the time goes in v8:
time: 113 us; the launch traced here: 112 us
  blocking collectives  90.7 us (80%)
  starting transfers between devices  11.6 us (10%)
  Pallas kernels  5.18 us (5%)
  waiting for transfers between devices  2.38 us (2%)
  local copies, waits for them, and re-layouts  1.54 us (1%)
    all_to_all x4, blocking collectives, swap(): return lax.all_to_all(rows, axis, split_axis=0, concat_axis=0, tiled=True)  90.7 us
    ppermute x2, starting transfers between devices, exchange(): return (received, lax.ppermute(received, 'core', [(0, 1), (1, 0)]))  11.6 us
    pallas_call x2, Pallas kernels, tile_sums(): call(sum_body, (jax.ShapeDtypeStruct((cuts, ROWS, width), BF16), jax.Shap...  2.62 us
    ppermute x2, waiting for transfers between devices, exchange(): return (received, lax.ppermute(received, 'core', [(0, 1), (1, 0)]))  2.38 us
  transfers between devices with their start and end apart: 2, of which 2 were waited for; matrix products, arithmetic and copies ran while one was open for 0% of the time, Pallas kernels for 0%

profile of v8, /device:TPU:1, one launch (start us, length us, event | category | flops | bytes accessed | tf_op | source)
XLA Modules:
  0.0 112.2 jit_solution(4757619913807312321)
XLA Ops:
  0.0 0.0 copy-start.4
  0.0 0.0 copy-start.5
  0.1 0.8 copy-done.1
  0.9 0.8 shard_map.120
  1.7 0.0 copy-start
  1.7 38.2 %all_to_all.20.received = bf16[64,48,128]{2,1,0:T(8,128)(2,1)S(1)} all-to-all(bf16[64,48,128]{2,1,0:T(8,128)(2,1)S(1)} %get-tuple-element.16), channel_id=1, replica_groups=mesh['chip'=64,'core'=2,'cuts'=4] {'chip'}, dimensions={0} | all-to-all | bytes 1572864 | tf_op jit(solution)/shard_map/all_to_all | solution.py:219
  40.0 5.3 %collective-permute-start = (bf16[64,48,128]{2,1,0:T(8,128)(2,1)S(1)}, bf16[64,48,128]{2,1,0:T(8,128)(2,1)S(1)}, u32[]{:S(2)}, u32[]{:S(2)}) collective-permute-start(bf16[64,48,128]{2,1,0:T(8,128)(2,1)S(1)} %all_to_all.20.received), channel_id=1, source_target_pairs={{0,4},{4,0},{1,5},{5,1},{2,6},{6,2},{3,7},{7,3},{8,12},{12,8},{9,1... | collective-permute-start | bytes 2359304 | tf_op jit(solution)/shard_map/ppermute | solution.py:224
  45.9 0.0 copy-start.9
  45.9 0.0 copy-start.10
  46.0 0.6 copy-done.9
  46.6 0.0 copy-done.10
  46.6 0.1 shard_map.118
  46.7 0.5 collective-permute-done.passed
  47.2 1.0 shard_map.121
  48.2 11.0 %all_to_all.21.parts = bf16[4,384,128]{2,1,0:T(8,128)(2,1)S(1)} all-to-all(bf16[4,384,128]{2,1,0:T(8,128)(2,1)S(1)} %get-tuple-element.17), channel_id=1, replica_groups=mesh['chip'=64,'core'=2,'cuts'=4] {'cuts'}, dimensions={0} | all-to-all | bytes 786432 | tf_op jit(solution)/shard_map/all_to_all | solution.py:219
  59.2 0.7 shard_map.122
  59.9 0.0 copy-start.3
  59.9 26.8 %all_to_all.22.received = bf16[64,48,128]{2,1,0:T(8,128)(2,1)S(1)} all-to-all(bf16[64,48,128]{2,1,0:T(8,128)(2,1)S(1)} %get-tuple-element.22), channel_id=1, replica_groups=mesh['chip'=64,'core'=2,'cuts'=4] {'chip'}, dimensions={0} | all-to-all | bytes 1572864 | tf_op jit(solution)/shard_map/all_to_all | solution.py:219
  86.7 6.3 %collective-permute-start.1 = (bf16[64,48,128]{2,1,0:T(8,128)(2,1)S(1)}, bf16[64,48,128]{2,1,0:T(8,128)(2,1)S(1)}, u32[]{:S(2)}, u32[]{:S(2)}) collective-permute-start(bf16[64,48,128]{2,1,0:T(8,128)(2,1)S(1)} %all_to_all.22.received), channel_id=1, source_target_pairs={{0,4},{4,0},{1,5},{5,1},{2,6},{6,2},{3,7},{7,3},{8,12},{12,8},{9,1... | collective-permute-start | bytes 2359304 | tf_op jit(solution)/shard_map/ppermute | solution.py:224
  93.1 1.9 %collective-permute-done.1.passed = bf16[64,48,128]{2,1,0:T(8,128)(2,1)S(1)} collective-permute-done((bf16[64,48,128]{2,1,0:T(8,128)(2,1)S(1)}, bf16[64,48,128]{2,1,0:T(8,128)(2,1)S(1)}, u32[]{:S(2)}, u32[]{:S(2)}) %collective-permute-start.1) | collective-permute-done | bytes 786464 | tf_op jit(solution)/shard_map/ppermute | solution.py:224
  94.9 1.6 %shard_map.123 = (bf16[4,384,256]{2,1,0:T(8,128)(2,1)S(1)}, f32[384,256]{1,0:T(8,128)S(1)}) custom-call(s32[128]{0:T(128)S(1)} %bitcast.15, bf16[384,128]{1,0:T(8,128)(2,1)S(1)} %get-tuple-element.21.own, bf16[64,48,128]{2,1,0:T(8,128)(2,1)S(1)} %all_to_all.22.received, bf16[64,48,128]{2,1,0:T(8,128)(2,1)S(1)} %collective-permute-done.1.passed, ...), custom_call_target="tpu_custom_call" | custom-call | tf_op jit(solution)/shard_map/pallas_call | solution.py:171
  96.6 0.0 copy-start.2
  96.6 14.6 %all_to_all.23.parts = bf16[4,384,256]{2,1,0:T(8,128)(2,1)S(1)} all-to-all(bf16[4,384,256]{2,1,0:T(8,128)(2,1)S(1)} %get-tuple-element.24), channel_id=1, replica_groups=mesh['chip'=64,'core'=2,'cuts'=4] {'cuts'}, dimensions={0} | all-to-all | bytes 1572864 | tf_op jit(solution)/shard_map/all_to_all | solution.py:219
  111.2 1.0 shard_map.124
  (13 shorter events, 0.0 us)
Async XLA Ops:
  0.0 0.9 copy-start.1
  0.0 0.9 copy-start.6
  0.0 0.9 copy-start.7
  0.0 0.9 copy-start.8
  0.0 0.9 copy-start.4
  0.0 0.9 copy-start.5
  1.7 45.5 %copy-start = (bf16[1,1,16,128,128]{4,3,2,1,0:T(8,128)(2,1)S(1)}, bf16[1,1,16,128,128]{4,3,2,1,0:T(8,128)(2,1)}, u32[]{:S(2)}) copy-start(bf16[1,1,16,128,128]{4,3,2,1,0:T(8,128)(2,1)} %param.23) | copy-start | bytes 1572868
  40.0 7.2 %collective-permute-start = (bf16[64,48,128]{2,1,0:T(8,128)(2,1)S(1)}, bf16[64,48,128]{2,1,0:T(8,128)(2,1)S(1)}, u32[]{:S(2)}, u32[]{:S(2)}) collective-permute-start(bf16[64,48,128]{2,1,0:T(8,128)(2,1)S(1)} %all_to_all.20.received), channel_id=1, source_target_pairs={{0,4},{4,0},{1,5},{5,1},{2,6},{6,2},{3,7},{7,3},{8,12},{12,8},{9,1... | collective-permute-start | bytes 2359304 | tf_op jit(solution)/shard_map/ppermute | solution.py:224
  45.9 0.7 copy-start.9
  45.9 0.7 copy-start.10
  59.9 35.0 %copy-start.3 = (bf16[128,256]{1,0:T(8,128)(2,1)S(1)}, bf16[128,256]{1,0:T(8,128)(2,1)}, u32[]{:S(2)}) copy-start(bf16[128,256]{1,0:T(8,128)(2,1)} %rest_0_.1) | copy-start | bytes 196612
  86.7 8.2 %collective-permute-start.1 = (bf16[64,48,128]{2,1,0:T(8,128)(2,1)S(1)}, bf16[64,48,128]{2,1,0:T(8,128)(2,1)S(1)}, u32[]{:S(2)}, u32[]{:S(2)}) collective-permute-start(bf16[64,48,128]{2,1,0:T(8,128)(2,1)S(1)} %all_to_all.22.received), channel_id=1, source_target_pairs={{0,4},{4,0},{1,5},{5,1},{2,6},{6,2},{3,7},{7,3},{8,12},{12,8},{9,1... | collective-permute-start | bytes 2359304 | tf_op jit(solution)/shard_map/ppermute | solution.py:224
  96.6 14.6 %copy-start.2 = (bf16[256,256]{1,0:T(8,128)(2,1)S(1)}, bf16[256,256]{1,0:T(8,128)(2,1)}, u32[]{:S(2)}) copy-start(bf16[256,256]{1,0:T(8,128)(2,1)} %weight.1) | copy-start | bytes 393220

commit v9 on v8

--- a/solution.py
+++ b/solution.py
@@ -62,9 +62,10 @@
         if dead != 0.0:
             rows = jnp.where(wide[:, :width] < 0, dead, rows)
         chips = pl.ds(first // CORES, CHUNK // CORES)
-        out[chips, : CORES * slots] = rows.astype(BF16).reshape(
-            CHUNK // CORES, CORES * slots, width
-        )
+        pairs = rows.astype(BF16).reshape(CHUNK // CORES, CORES, slots, width)
+        core = lax.axis_index("core")
+        out[chips, :slots] = jnp.where(core == 0, pairs[:, 0], pairs[:, 1])
+        out[chips, slots : CORES * slots] = jnp.where(core == 0, pairs[:, 1], pairs[:, 0])
         out[chips, CORES * slots :] = jnp.broadcast_to(
             hubs[None], (CHUNK // CORES,) + hubs.shape
         )
@@ -142,8 +143,8 @@
         away = jnp.maximum(col - own_blocks, 0)
         hub = jnp.where(away >= groups, 1, 0)
         first = pl.multiple_of((away - hub * groups) * group, group)
-        start = pl.multiple_of(jnp.where(hub == 1, CORES * SLOT, core * SLOT), SLOT)
-        same = received[pl.ds(first, group), pl.ds(start, SLOT), :]
+        start = pl.multiple_of(hub * SLOT, SLOT)
+        same = received[pl.ds(first, group), pl.ds(pl.multiple_of(start * CORES, SLOT), SLOT), :]
         other = passed[pl.ds(first, group), pl.ds(start, SLOT), :]
         remote_rows = jnp.stack(
             [jnp.where(core == 0, same, other), jnp.where(core == 0, other, same)],
@@ -221,7 +222,7 @@
 
 def exchange(rows):
     received = swap(rows, "chip")
-    return received, lax.ppermute(received, "core", [(0, 1), (1, 0)])
+    return received, lax.ppermute(received[:, SLOT:], "core", [(0, 1), (1, 0)])
 
 
 def local(

time: 113 us -> 112 us (level)
  no operation moved by 1% of the time
where the time goes in v9:
time: 112 us; the launch traced here: 111 us
  blocking collectives  90.4 us (81%)
  starting transfers between devices  11.8 us (11%)
  Pallas kernels  5.17 us (5%)
  waiting for transfers between devices  1.63 us (1%)
  local copies, waits for them, and re-layouts  1.61 us (1%)
    all_to_all x4, blocking collectives, swap(): return lax.all_to_all(rows, axis, split_axis=0, concat_axis=0, tiled=True)  90.4 us
    ppermute x2, starting transfers between devices, exchange(): lax.ppermute(received[:, SLOT:], 'core', [(0, 1), (1, 0)])  11.8 us
    pallas_call x2, Pallas kernels, tile_sums(): call(sum_body, (jax.ShapeDtypeStruct((cuts, ROWS, width), BF16), jax.Shap...  2.61 us
  transfers between devices with their start and end apart: 2, of which 2 were waited for; matrix products, arithmetic and copies ran while one was open for 0% of the time, Pallas kernels for 0%

profile of v9, /device:TPU:1, one launch (start us, length us, event | category | flops | bytes accessed | tf_op | source)
XLA Modules:
  0.0 111.4 jit_solution(1316427086938947488)
XLA Ops:
  0.0 0.0 copy-start.8
  0.0 0.0 copy-start.4
  0.0 0.0 copy-start.5
  0.1 0.8 copy-done.1
  0.9 0.8 shard_map.120
  1.7 38.1 %all_to_all.20.received = bf16[64,48,128]{2,1,0:T(8,128)(2,1)S(1)} all-to-all(bf16[64,48,128]{2,1,0:T(8,128)(2,1)S(1)} %get-tuple-element.16), channel_id=1, replica_groups=mesh['chip'=64,'core'=2,'cuts'=4] {'chip'}, dimensions={0} | all-to-all | bytes 1572864 | tf_op jit(solution)/shard_map/all_to_all | solution.py:220
  39.9 5.5 %collective-permute-start = (bf16[64,32,128]{2,1,0:T(8,128)(2,1)S(1)}, bf16[64,32,128]{2,1,0:T(8,128)(2,1)S(1)}, u32[]{:S(2)}, u32[]{:S(2)}) collective-permute-start(bf16[64,32,128]{2,1,0:T(8,128)(2,1)S(1)} %slice.8), channel_id=1, source_target_pairs={{0,4},{4,0},{1,5},{5,1},{2,6},{6,2},{3,7},{7,3},{8,12},{12,8},{9,1... | collective-permute-start | bytes 1572872 | tf_op jit(solution)/shard_map/ppermute | solution.py:225
  46.0 0.0 copy-start.9
  46.0 0.0 copy-start.10
  46.0 0.6 copy-done.9
  46.6 0.0 copy-done.10
  46.7 0.1 shard_map.118
  46.7 0.1 collective-permute-done.passed
  46.8 1.0 shard_map.121
  47.8 11.0 %all_to_all.21.parts = bf16[4,384,128]{2,1,0:T(8,128)(2,1)S(1)} all-to-all(bf16[4,384,128]{2,1,0:T(8,128)(2,1)S(1)} %get-tuple-element.17), channel_id=1, replica_groups=mesh['chip'=64,'core'=2,'cuts'=4] {'cuts'}, dimensions={0} | all-to-all | bytes 786432 | tf_op jit(solution)/shard_map/all_to_all | solution.py:220
  58.9 0.7 shard_map.122
  59.6 26.7 %all_to_all.22.received = bf16[64,48,128]{2,1,0:T(8,128)(2,1)S(1)} all-to-all(bf16[64,48,128]{2,1,0:T(8,128)(2,1)S(1)} %get-tuple-element.22), channel_id=1, replica_groups=mesh['chip'=64,'core'=2,'cuts'=4] {'chip'}, dimensions={0} | all-to-all | bytes 1572864 | tf_op jit(solution)/shard_map/all_to_all | solution.py:220
  86.3 6.3 %collective-permute-start.1 = (bf16[64,32,128]{2,1,0:T(8,128)(2,1)S(1)}, bf16[64,32,128]{2,1,0:T(8,128)(2,1)S(1)}, u32[]{:S(2)}, u32[]{:S(2)}) collective-permute-start(bf16[64,32,128]{2,1,0:T(8,128)(2,1)S(1)} %slice.9), channel_id=1, source_target_pairs={{0,4},{4,0},{1,5},{5,1},{2,6},{6,2},{3,7},{7,3},{8,12},{12,8},{9,1... | collective-permute-start | bytes 1572872 | tf_op jit(solution)/shard_map/ppermute | solution.py:225
  92.6 1.5 %collective-permute-done.1.passed = bf16[64,32,128]{2,1,0:T(8,128)(2,1)S(1)} collective-permute-done((bf16[64,32,128]{2,1,0:T(8,128)(2,1)S(1)}, bf16[64,32,128]{2,1,0:T(8,128)(2,1)S(1)}, u32[]{:S(2)}, u32[]{:S(2)}) %collective-permute-start.1) | collective-permute-done | bytes 524320 | tf_op jit(solution)/shard_map/ppermute | solution.py:225
  94.1 1.6 %shard_map.123 = (bf16[4,384,256]{2,1,0:T(8,128)(2,1)S(1)}, f32[384,256]{1,0:T(8,128)S(1)}) custom-call(s32[128]{0:T(128)S(1)} %bitcast.15, bf16[384,128]{1,0:T(8,128)(2,1)S(1)} %get-tuple-element.21.own, bf16[64,48,128]{2,1,0:T(8,128)(2,1)S(1)} %all_to_all.22.received, bf16[64,32,128]{2,1,0:T(8,128)(2,1)S(1)} %collective-permute-done.1.passed, ...), custom_call_target="tpu_custom_call" | custom-call | tf_op jit(solution)/shard_map/pallas_call | solution.py:172
  95.8 0.0 copy-start.2
  95.8 14.6 %all_to_all.23.parts = bf16[4,384,256]{2,1,0:T(8,128)(2,1)S(1)} all-to-all(bf16[4,384,256]{2,1,0:T(8,128)(2,1)S(1)} %get-tuple-element.24), channel_id=1, replica_groups=mesh['chip'=64,'core'=2,'cuts'=4] {'cuts'}, dimensions={0} | all-to-all | bytes 1572864 | tf_op jit(solution)/shard_map/all_to_all | solution.py:220
  110.4 0.0 copy-done.2
  110.4 1.0 shard_map.124
  (15 shorter events, 0.1 us)
Async XLA Ops:
  0.0 0.9 copy-start.1
  0.0 0.9 copy-start.6
  0.0 0.9 copy-start.7
  0.0 0.9 copy-start.8
  0.0 0.9 copy-start.4
  0.0 0.9 copy-start.5
  39.8 7.0 %copy-start = (bf16[1,1,16,128,128]{4,3,2,1,0:T(8,128)(2,1)S(1)}, bf16[1,1,16,128,128]{4,3,2,1,0:T(8,128)(2,1)}, u32[]{:S(2)}) copy-start(bf16[1,1,16,128,128]{4,3,2,1,0:T(8,128)(2,1)} %param.23) | copy-start | bytes 1572868
  39.9 7.0 %collective-permute-start = (bf16[64,32,128]{2,1,0:T(8,128)(2,1)S(1)}, bf16[64,32,128]{2,1,0:T(8,128)(2,1)S(1)}, u32[]{:S(2)}, u32[]{:S(2)}) collective-permute-start(bf16[64,32,128]{2,1,0:T(8,128)(2,1)S(1)} %slice.8), channel_id=1, source_target_pairs={{0,4},{4,0},{1,5},{5,1},{2,6},{6,2},{3,7},{7,3},{8,12},{12,8},{9,1... | collective-permute-start | bytes 1572872 | tf_op jit(solution)/shard_map/ppermute | solution.py:225
  46.0 0.7 copy-start.9
  46.0 0.7 copy-start.10
  86.3 7.9 %copy-start.3 = (bf16[128,256]{1,0:T(8,128)(2,1)S(1)}, bf16[128,256]{1,0:T(8,128)(2,1)}, u32[]{:S(2)}) copy-start(bf16[128,256]{1,0:T(8,128)(2,1)} %rest_0_.1) | copy-start | bytes 196612
  86.3 7.8 %collective-permute-start.1 = (bf16[64,32,128]{2,1,0:T(8,128)(2,1)S(1)}, bf16[64,32,128]{2,1,0:T(8,128)(2,1)S(1)}, u32[]{:S(2)}, u32[]{:S(2)}) collective-permute-start(bf16[64,32,128]{2,1,0:T(8,128)(2,1)S(1)} %slice.9), channel_id=1, source_target_pairs={{0,4},{4,0},{1,5},{5,1},{2,6},{6,2},{3,7},{7,3},{8,12},{12,8},{9,1... | collective-permute-start | bytes 1572872 | tf_op jit(solution)/shard_map/ppermute | solution.py:225
  95.8 14.6 %copy-start.2 = (bf16[256,256]{1,0:T(8,128)(2,1)S(1)}, bf16[256,256]{1,0:T(8,128)(2,1)}, u32[]{:S(2)}) copy-start(bf16[256,256]{1,0:T(8,128)(2,1)} %weight.1) | copy-start | bytes 393220

commit v10 on v9

--- a/solution.py
+++ b/solution.py
@@ -1,3 +1,5 @@
+import functools
+
 import jax
 import jax.numpy as jnp
 from jax import lax
@@ -11,6 +13,7 @@
 BLOCK = 128
 CHUNK = 16
 CORES = 2
+HIDDEN_ROWS = 512
 DEAD = 2.0**100
 DEAD_LIMIT = 2.0**50
 VMEM = pltpu.VMEM
@@ -127,8 +130,8 @@
     )(targets, columns, used)
 
 
-def sum_body(plan, own, received, passed, tiles, *rest):
-    *layer, out, mine, total = rest
+def sum_body(layers, plan, own, received, passed, tiles, *rest):
+    layer, (out, mine, total, *scratch) = rest[:layers], rest[layers:]
     total[...] = jnp.zeros_like(total)
     capacity = tiles.shape[0]
     group = BLOCK // (CORES * SLOT)
@@ -136,7 +139,8 @@
     core = lax.axis_index("core")
     own_blocks = ROWS // BLOCK
     used = plan[2 * capacity]
-    for i in range(capacity):
+
+    def source_rows(i):
         col = plan[capacity + i]
         here = jnp.minimum(col, own_blocks - 1)
         local_rows = own[pl.ds(pl.multiple_of(here * BLOCK, BLOCK), BLOCK), :]
@@ -150,14 +154,22 @@
             [jnp.where(core == 0, same, other), jnp.where(core == 0, other, same)],
             axis=1,
         ).reshape(BLOCK, own.shape[1])
-        rows = jnp.where(col < own_blocks, local_rows, remote_rows)
-        if layer:
-            weight, bias = layer
+        return jnp.where(col < own_blocks, local_rows, remote_rows)
+
+    if layer:
+        (weight, bias), (picked, values) = layer, scratch
+        for i in range(capacity):
+            picked[i * BLOCK : (i + 1) * BLOCK] = source_rows(i)
+        for first in range(0, capacity * BLOCK, HIDDEN_ROWS):
+            span = pl.ds(first, HIDDEN_ROWS)
+            rows = picked[span]
             hidden = jnp.dot(rows, weight[...], preferred_element_type=F32)
             hidden = jnp.maximum(hidden + bias[...], 0.0)
             live = rows.astype(F32) < DEAD_LIMIT
             live = jnp.concatenate([live] * (hidden.shape[1] // live.shape[1]), axis=1)
-            rows = jnp.where(live, hidden, 0.0).astype(BF16)
+            values[span] = jnp.where(live, hidden, 0.0).astype(BF16)
+    for i in range(capacity):
+        rows = values[i * BLOCK : (i + 1) * BLOCK] if layer else source_rows(i)
         term = jnp.dot(tiles[i], rows, preferred_element_type=F32)
         row = plan[i]
         total[row] = total[row] + jnp.where(i < used, term, 0.0)
@@ -169,14 +181,18 @@
 
 def tile_sums(own, received, passed, plan, tiles, cuts, *layer):
     width = layer[0].shape[1] if layer else own.shape[1]
-    return call(
-        sum_body,
+    rows = tiles.shape[0] * BLOCK
+    scratch = [pltpu.VMEM((cuts * ROWS // BLOCK, BLOCK, width), F32)]
+    if layer:
+        scratch += [pltpu.VMEM((rows, own.shape[1]), BF16), pltpu.VMEM((rows, width), BF16)]
+    return call(
+        functools.partial(sum_body, len(layer)),
         (
             jax.ShapeDtypeStruct((cuts, ROWS, width), BF16),
             jax.ShapeDtypeStruct((ROWS, width), F32),
         ),
         [SMEM] + [VMEM] * (4 + len(layer)),
-        [pltpu.VMEM((cuts * ROWS // BLOCK, BLOCK, width), F32)],
+        scratch,
     )(plan, own, received, passed, tiles, *layer)
 
 

time: 112 us -> 112 us (level)
  no operation moved by 1% of the time
where the time goes in v10:
time: 112 us; the launch traced here: 111 us
  blocking collectives  90.4 us (81%)
  starting transfers between devices  11.8 us (11%)
  Pallas kernels  5.06 us (5%)
  waiting for transfers between devices  1.63 us (1%)
  local copies, waits for them, and re-layouts  1.61 us (1%)
    all_to_all x4, blocking collectives, swap(): return lax.all_to_all(rows, axis, split_axis=0, concat_axis=0, tiled=True)  90.4 us
    ppermute x2, starting transfers between devices, exchange(): lax.ppermute(received[:, SLOT:], 'core', [(0, 1), (1, 0)])  11.8 us
    pallas_call x2, Pallas kernels, tile_sums(): call(functools.partial(sum_body, len(layer)), (jax.ShapeDtypeStruct((cuts...  2.49 us
  transfers between devices with their start and end apart: 2, of which 2 were waited for; matrix products, arithmetic and copies ran while one was open for 0% of the time, Pallas kernels for 0%

profile of v10, /device:TPU:1, one launch (start us, length us, event | category | flops | bytes accessed | tf_op | source)
XLA Modules:
  0.0 111.3 jit_solution(6256157164428164908)
XLA Ops:
  0.0 0.0 copy-start.8
  0.0 0.0 copy-start.4
  0.0 0.0 copy-start.5
  0.1 0.8 copy-done.1
  0.9 0.0 copy-done.8
  0.9 0.8 shard_map.120
  1.7 38.1 %all_to_all.20.received = bf16[64,48,128]{2,1,0:T(8,128)(2,1)S(1)} all-to-all(bf16[64,48,128]{2,1,0:T(8,128)(2,1)S(1)} %get-tuple-element.16), channel_id=1, replica_groups=mesh['chip'=64,'core'=2,'cuts'=4] {'chip'}, dimensions={0} | all-to-all | bytes 1572864 | tf_op jit(solution)/shard_map/all_to_all | solution.py:236
  39.9 5.5 %collective-permute-start = (bf16[64,32,128]{2,1,0:T(8,128)(2,1)S(1)}, bf16[64,32,128]{2,1,0:T(8,128)(2,1)S(1)}, u32[]{:S(2)}, u32[]{:S(2)}) collective-permute-start(bf16[64,32,128]{2,1,0:T(8,128)(2,1)S(1)} %slice.8), channel_id=1, source_target_pairs={{0,4},{4,0},{1,5},{5,1},{2,6},{6,2},{3,7},{7,3},{8,12},{12,8},{9,1... | collective-permute-start | bytes 1572872 | tf_op jit(solution)/shard_map/ppermute | solution.py:241
  46.0 0.0 copy-start.9
  46.0 0.0 copy-start.10
  46.0 0.6 copy-done.9
  46.6 0.0 copy-done.10
  46.7 0.1 shard_map.118
  46.7 0.1 collective-permute-done.passed
  46.8 1.0 shard_map.121
  47.8 11.0 %all_to_all.21.parts = bf16[4,384,128]{2,1,0:T(8,128)(2,1)S(1)} all-to-all(bf16[4,384,128]{2,1,0:T(8,128)(2,1)S(1)} %get-tuple-element.17), channel_id=1, replica_groups=mesh['chip'=64,'core'=2,'cuts'=4] {'cuts'}, dimensions={0} | all-to-all | bytes 786432 | tf_op jit(solution)/shard_map/all_to_all | solution.py:236
  58.9 0.7 shard_map.122
  59.5 26.7 %all_to_all.22.received = bf16[64,48,128]{2,1,0:T(8,128)(2,1)S(1)} all-to-all(bf16[64,48,128]{2,1,0:T(8,128)(2,1)S(1)} %get-tuple-element.22), channel_id=1, replica_groups=mesh['chip'=64,'core'=2,'cuts'=4] {'chip'}, dimensions={0} | all-to-all | bytes 1572864 | tf_op jit(solution)/shard_map/all_to_all | solution.py:236
  86.3 6.3 %collective-permute-start.1 = (bf16[64,32,128]{2,1,0:T(8,128)(2,1)S(1)}, bf16[64,32,128]{2,1,0:T(8,128)(2,1)S(1)}, u32[]{:S(2)}, u32[]{:S(2)}) collective-permute-start(bf16[64,32,128]{2,1,0:T(8,128)(2,1)S(1)} %slice.9), channel_id=1, source_target_pairs={{0,4},{4,0},{1,5},{5,1},{2,6},{6,2},{3,7},{7,3},{8,12},{12,8},{9,1... | collective-permute-start | bytes 1572872 | tf_op jit(solution)/shard_map/ppermute | solution.py:241
  92.6 1.5 %collective-permute-done.1.passed = bf16[64,32,128]{2,1,0:T(8,128)(2,1)S(1)} collective-permute-done((bf16[64,32,128]{2,1,0:T(8,128)(2,1)S(1)}, bf16[64,32,128]{2,1,0:T(8,128)(2,1)S(1)}, u32[]{:S(2)}, u32[]{:S(2)}) %collective-permute-start.1) | collective-permute-done | bytes 524320 | tf_op jit(solution)/shard_map/ppermute | solution.py:241
  94.1 1.5 %shard_map.123 = (bf16[4,384,256]{2,1,0:T(8,128)(2,1)S(1)}, f32[384,256]{1,0:T(8,128)S(1)}) custom-call(s32[128]{0:T(128)S(1)} %bitcast.15, bf16[384,128]{1,0:T(8,128)(2,1)S(1)} %get-tuple-element.21.own, bf16[64,48,128]{2,1,0:T(8,128)(2,1)S(1)} %all_to_all.22.received, bf16[64,32,128]{2,1,0:T(8,128)(2,1)S(1)} %collective-permute-done.1.passed, ...), custom_call_target="tpu_custom_call" | custom-call | tf_op jit(solution)/shard_map/pallas_call | solution.py:188
  95.7 0.0 copy-start.2
  95.7 14.6 %all_to_all.23.parts = bf16[4,384,256]{2,1,0:T(8,128)(2,1)S(1)} all-to-all(bf16[4,384,256]{2,1,0:T(8,128)(2,1)S(1)} %get-tuple-element.24), channel_id=1, replica_groups=mesh['chip'=64,'core'=2,'cuts'=4] {'cuts'}, dimensions={0} | all-to-all | bytes 1572864 | tf_op jit(solution)/shard_map/all_to_all | solution.py:236
  110.3 1.0 shard_map.124
  (15 shorter events, 0.1 us)
Async XLA Ops:
  0.0 0.9 copy-start.1
  0.0 0.9 copy-start.6
  0.0 0.9 copy-start.7
  0.0 0.9 copy-start.8
  0.0 0.9 copy-start.4
  0.0 0.9 copy-start.5
  39.8 7.0 %copy-start = (bf16[1,1,16,128,128]{4,3,2,1,0:T(8,128)(2,1)S(1)}, bf16[1,1,16,128,128]{4,3,2,1,0:T(8,128)(2,1)}, u32[]{:S(2)}) copy-start(bf16[1,1,16,128,128]{4,3,2,1,0:T(8,128)(2,1)} %param.23) | copy-start | bytes 1572868
  39.9 7.0 %collective-permute-start = (bf16[64,32,128]{2,1,0:T(8,128)(2,1)S(1)}, bf16[64,32,128]{2,1,0:T(8,128)(2,1)S(1)}, u32[]{:S(2)}, u32[]{:S(2)}) collective-permute-start(bf16[64,32,128]{2,1,0:T(8,128)(2,1)S(1)} %slice.8), channel_id=1, source_target_pairs={{0,4},{4,0},{1,5},{5,1},{2,6},{6,2},{3,7},{7,3},{8,12},{12,8},{9,1... | collective-permute-start | bytes 1572872 | tf_op jit(solution)/shard_map/ppermute | solution.py:241
  46.0 0.7 copy-start.9
  46.0 0.7 copy-start.10
  86.3 7.9 %copy-start.3 = (bf16[128,256]{1,0:T(8,128)(2,1)S(1)}, bf16[128,256]{1,0:T(8,128)(2,1)}, u32[]{:S(2)}) copy-start(bf16[128,256]{1,0:T(8,128)(2,1)} %rest_0_.1) | copy-start | bytes 196612
  86.3 7.8 %collective-permute-start.1 = (bf16[64,32,128]{2,1,0:T(8,128)(2,1)S(1)}, bf16[64,32,128]{2,1,0:T(8,128)(2,1)S(1)}, u32[]{:S(2)}, u32[]{:S(2)}) collective-permute-start(bf16[64,32,128]{2,1,0:T(8,128)(2,1)S(1)} %slice.9), channel_id=1, source_target_pairs={{0,4},{4,0},{1,5},{5,1},{2,6},{6,2},{3,7},{7,3},{8,12},{12,8},{9,1... | collective-permute-start | bytes 1572872 | tf_op jit(solution)/shard_map/ppermute | solution.py:241
  95.7 14.6 %copy-start.2 = (bf16[256,256]{1,0:T(8,128)(2,1)S(1)}, bf16[256,256]{1,0:T(8,128)(2,1)}, u32[]{:S(2)}) copy-start(bf16[256,256]{1,0:T(8,128)(2,1)} %weight.1) | copy-start | bytes 393220

commit v11 on v9

--- a/solution.py
+++ b/solution.py
@@ -114,17 +114,24 @@
     )(*handed, *operands)
 
 
-def plan_body(targets, columns, used, out):
+def plan_body(targets, columns, used, first, second, out, first_out, second_out):
     capacity = targets.shape[1]
     out[...] = jnp.broadcast_to(used[...], out.shape)
     out[:, :capacity] = targets[...]
     out[:, capacity : 2 * capacity] = columns[...]
-
-
-def tile_plan(targets, columns, used):
-    return call(
-        plan_body, jax.ShapeDtypeStruct((1, 128), jnp.int32), [VMEM] * 3
-    )(targets, columns, used)
+    first_out[...] = first[...]
+    second_out[...] = second[...]
+
+
+def tile_plan(targets, columns, used, *biases):
+    return call(
+        plan_body,
+        (
+            jax.ShapeDtypeStruct((1, 128), jnp.int32),
+            *(jax.ShapeDtypeStruct(x.shape, x.dtype) for x in biases),
+        ),
+        [VMEM] * 5,
+    )(targets, columns, used, *biases)
 
 
 def sum_body(plan, own, received, passed, tiles, *rest):
@@ -243,14 +250,13 @@
     halo_rows = halo_rows.reshape(halo_rows.shape[2:]).T
     tiles = tile_values.reshape(tile_values.shape[2:])
     row = lambda x: x.reshape(1, -1)
-    outgoing, picks, hub_picks, bias_one, bias_two = pack(
-        (row(bias_one), row(bias_two)),
-        halo_rows,
-        row(halo_count),
-        row(hub_rows),
-        features,
-    )
-    plan = tile_plan(row(tile_target), row(tile_source), row(tile_count)).reshape(-1)
+    outgoing, picks, hub_picks = pack(
+        (), halo_rows, row(halo_count), row(hub_rows), features
+    )
+    plan, bias_one, bias_two = tile_plan(
+        row(tile_target), row(tile_source), row(tile_count), row(bias_one), row(bias_two)
+    )
+    plan = plan.reshape(-1)
     parts, mine = tile_sums(features, *exchange(outgoing), plan, tiles, cuts)
     table, outgoing = middle(swap(parts, "cuts"), mine, picks, hub_picks)
     parts, mine = tile_sums(

time: 112 us -> 112 us (level)
  no operation moved by 1% of the time
where the time goes in v11:
time: 112 us; the launch traced here: 111 us
  blocking collectives  90.4 us (81%)
  starting transfers between devices  11.8 us (11%)
  Pallas kernels  5.16 us (5%)
  local copies, waits for them, and re-layouts  1.62 us (1%)
  waiting for transfers between devices  1.62 us (1%)
    all_to_all x4, blocking collectives, swap(): return lax.all_to_all(rows, axis, split_axis=0, concat_axis=0, tiled=True)  90.4 us
    ppermute x2, starting transfers between devices, exchange(): lax.ppermute(received[:, SLOT:], 'core', [(0, 1), (1, 0)])  11.8 us
    pallas_call x2, Pallas kernels, tile_sums(): call(sum_body, (jax.ShapeDtypeStruct((cuts, ROWS, width), BF16), jax.Shap...  2.59 us
  transfers between devices with their start and end apart: 2, of which 2 were waited for; matrix products, arithmetic and copies ran while one was open for 0% of the time, Pallas kernels for 0%

profile of v11, /device:TPU:1, one launch (start us, length us, event | category | flops | bytes accessed | tf_op | source)
XLA Modules:
  0.0 111.4 jit_solution(2533903741733074864)
XLA Ops:
  0.0 0.0 copy-start.7
  0.0 0.0 copy-start.8
  0.0 0.9 copy-done.1
  0.9 0.0 copy-done.4
  0.9 0.0 copy-done.7
  0.9 0.8 shard_map.120
  1.7 38.1 %all_to_all.20.received = bf16[64,48,128]{2,1,0:T(8,128)(2,1)S(1)} all-to-all(bf16[64,48,128]{2,1,0:T(8,128)(2,1)S(1)} %get-tuple-element.18), channel_id=1, replica_groups=mesh['chip'=64,'core'=2,'cuts'=4] {'chip'}, dimensions={0} | all-to-all | bytes 1572864 | tf_op jit(solution)/shard_map/all_to_all | solution.py:227
  39.8 5.5 %collective-permute-start = (bf16[64,32,128]{2,1,0:T(8,128)(2,1)S(1)}, bf16[64,32,128]{2,1,0:T(8,128)(2,1)S(1)}, u32[]{:S(2)}, u32[]{:S(2)}) collective-permute-start(bf16[64,32,128]{2,1,0:T(8,128)(2,1)S(1)} %slice.8), channel_id=1, source_target_pairs={{0,4},{4,0},{1,5},{5,1},{2,6},{6,2},{3,7},{7,3},{8,12},{12,8},{9,1... | collective-permute-start | bytes 1572872 | tf_op jit(solution)/shard_map/ppermute | solution.py:232
  46.0 0.0 copy-start.5
  46.0 0.0 copy-start.9
  46.0 0.6 copy-done.5
  46.7 0.1 shard_map.118
  46.7 0.1 collective-permute-done.passed
  46.8 1.0 shard_map.121
  47.8 11.0 %all_to_all.21.parts = bf16[4,384,128]{2,1,0:T(8,128)(2,1)S(1)} all-to-all(bf16[4,384,128]{2,1,0:T(8,128)(2,1)S(1)} %get-tuple-element.19), channel_id=1, replica_groups=mesh['chip'=64,'core'=2,'cuts'=4] {'cuts'}, dimensions={0} | all-to-all | bytes 786432 | tf_op jit(solution)/shard_map/all_to_all | solution.py:227
  58.9 0.7 shard_map.122
  59.6 26.7 %all_to_all.22.received = bf16[64,48,128]{2,1,0:T(8,128)(2,1)S(1)} all-to-all(bf16[64,48,128]{2,1,0:T(8,128)(2,1)S(1)} %get-tuple-element.24), channel_id=1, replica_groups=mesh['chip'=64,'core'=2,'cuts'=4] {'chip'}, dimensions={0} | all-to-all | bytes 1572864 | tf_op jit(solution)/shard_map/all_to_all | solution.py:227
  86.3 6.3 %collective-permute-start.1 = (bf16[64,32,128]{2,1,0:T(8,128)(2,1)S(1)}, bf16[64,32,128]{2,1,0:T(8,128)(2,1)S(1)}, u32[]{:S(2)}, u32[]{:S(2)}) collective-permute-start(bf16[64,32,128]{2,1,0:T(8,128)(2,1)S(1)} %slice.9), channel_id=1, source_target_pairs={{0,4},{4,0},{1,5},{5,1},{2,6},{6,2},{3,7},{7,3},{8,12},{12,8},{9,1... | collective-permute-start | bytes 1572872 | tf_op jit(solution)/shard_map/ppermute | solution.py:232
  92.6 1.5 %collective-permute-done.1.passed = bf16[64,32,128]{2,1,0:T(8,128)(2,1)S(1)} collective-permute-done((bf16[64,32,128]{2,1,0:T(8,128)(2,1)S(1)}, bf16[64,32,128]{2,1,0:T(8,128)(2,1)S(1)}, u32[]{:S(2)}, u32[]{:S(2)}) %collective-permute-start.1) | collective-permute-done | bytes 524320 | tf_op jit(solution)/shard_map/ppermute | solution.py:232
  94.1 1.6 %shard_map.123 = (bf16[4,384,256]{2,1,0:T(8,128)(2,1)S(1)}, f32[384,256]{1,0:T(8,128)S(1)}) custom-call(s32[128]{0:T(128)S(1)} %bitcast.15, bf16[384,128]{1,0:T(8,128)(2,1)S(1)} %get-tuple-element.23.own, bf16[64,48,128]{2,1,0:T(8,128)(2,1)S(1)} %all_to_all.22.received, bf16[64,32,128]{2,1,0:T(8,128)(2,1)S(1)} %collective-permute-done.1.passed, ...), custom_call_target="tpu_custom_call" | custom-call | tf_op jit(solution)/shard_map/pallas_call | solution.py:179
  95.8 0.0 copy-start.2
  95.8 14.6 %all_to_all.23.parts = bf16[4,384,256]{2,1,0:T(8,128)(2,1)S(1)} all-to-all(bf16[4,384,256]{2,1,0:T(8,128)(2,1)S(1)} %get-tuple-element.26), channel_id=1, replica_groups=mesh['chip'=64,'core'=2,'cuts'=4] {'cuts'}, dimensions={0} | all-to-all | bytes 1572864 | tf_op jit(solution)/shard_map/all_to_all | solution.py:227
  110.3 0.0 copy-done.2
  110.3 1.0 shard_map.124
  (15 shorter events, 0.1 us)
Async XLA Ops:
  0.0 0.9 copy-start.1
  0.0 0.9 copy-start.4
  0.0 0.9 copy-start.7
  0.0 0.9 copy-start.8
  39.8 6.2 %copy-start.6 = (f32[256]{0:T(256)S(1)}, f32[256]{0:T(256)}, u32[]{:S(2)}) copy-start(f32[256]{0:T(256)} %param.16) | copy-start | bytes 3076
  39.8 6.2 %copy-start.10 = (s32[1,1,16]{2,1,0:T(1,128)S(1)}, s32[1,1,16]{2,1,0:T(1,128)}, u32[]{:S(2)}) copy-start(s32[1,1,16]{2,1,0:T(1,128)} %param.21) | copy-start | bytes 196
  39.8 7.0 %copy-start = (bf16[1,1,16,128,128]{4,3,2,1,0:T(8,128)(2,1)S(1)}, bf16[1,1,16,128,128]{4,3,2,1,0:T(8,128)(2,1)}, u32[]{:S(2)}) copy-start(bf16[1,1,16,128,128]{4,3,2,1,0:T(8,128)(2,1)} %param.23) | copy-start | bytes 1572868
  39.8 7.0 %collective-permute-start = (bf16[64,32,128]{2,1,0:T(8,128)(2,1)S(1)}, bf16[64,32,128]{2,1,0:T(8,128)(2,1)S(1)}, u32[]{:S(2)}, u32[]{:S(2)}) collective-permute-start(bf16[64,32,128]{2,1,0:T(8,128)(2,1)S(1)} %slice.8), channel_id=1, source_target_pairs={{0,4},{4,0},{1,5},{5,1},{2,6},{6,2},{3,7},{7,3},{8,12},{12,8},{9,1... | collective-permute-start | bytes 1572872 | tf_op jit(solution)/shard_map/ppermute | solution.py:232
  46.0 0.7 copy-start.5
  46.0 0.7 copy-start.9
  86.2 7.9 %copy-start.3 = (bf16[128,256]{1,0:T(8,128)(2,1)S(1)}, bf16[128,256]{1,0:T(8,128)(2,1)}, u32[]{:S(2)}) copy-start(bf16[128,256]{1,0:T(8,128)(2,1)} %rest_0_.1) | copy-start | bytes 196612
  86.3 7.8 %collective-permute-start.1 = (bf16[64,32,128]{2,1,0:T(8,128)(2,1)S(1)}, bf16[64,32,128]{2,1,0:T(8,128)(2,1)S(1)}, u32[]{:S(2)}, u32[]{:S(2)}) collective-permute-start(bf16[64,32,128]{2,1,0:T(8,128)(2,1)S(1)} %slice.9), channel_id=1, source_target_pairs={{0,4},{4,0},{1,5},{5,1},{2,6},{6,2},{3,7},{7,3},{8,12},{12,8},{9,1... | collective-permute-start | bytes 1572872 | tf_op jit(solution)/shard_map/ppermute | solution.py:232
  95.8 14.6 %copy-start.2 = (bf16[256,256]{1,0:T(8,128)(2,1)S(1)}, bf16[256,256]{1,0:T(8,128)(2,1)}, u32[]{:S(2)}) copy-start(bf16[256,256]{1,0:T(8,128)(2,1)} %weight.1) | copy-start | bytes 393220
